TPU v7x, 256 devices: a whole 4x4x8 slice. The times are simulated.
256 devices in a mesh: grp: 32 (over z, y_hi, core), patch: 8 (over y_lo, x).
Axes of the slice: x: 4, y: 4 (y_hi: 2, y_lo: 2; y = y_hi * 2 + y_lo), z: 8, core: 2. Of those that a mesh axis runs over, the one named last changes fastest.
Arguments:
- latent: bfloat16 [32768, 1536], P(('grp', 'patch')), may hold values from -24 to 24
- incoming: int32 [8, 32], P('patch', 'grp'), may hold values from 0 to 31, each once within a row
- req_pages: int32 [32, 4], P('grp'), may hold values from 1 to 48, 64 in all within a row
- text_len: int32 [32, 4], P('grp'), may hold values from 1 to 128, as said below
- gate_scale: float32 [32, 4, 1536], P('grp'), may hold values from 0.2 to 1.2
- text_keys: bfloat16 [32, 4, 128, 1536], P('grp'), may hold values from -6 to 6
- text_values: bfloat16 [32, 4, 128, 1536], P('grp'), may hold values from -6 to 6
- w_query: bfloat16 [1536, 1536], P('grp'), may hold values from -0.25 to 0.25
- w_key: bfloat16 [1536, 1536], P('grp'), may hold values from -0.25 to 0.25
- w_value: bfloat16 [1536, 1536], P('grp'), may hold values from -0.15625 to 0.15625
- w_out: bfloat16 [1536, 1536], replicated, may hold values from -0.15625 to 0.15625
Outputs:
- denoised: bfloat16 [32768, 1536], P(('grp', 'patch'))
Inputs may be any that keep to these rules, and one draw needn't show every extreme that they name: `incoming`: each row is a permutation. `req_pages`: A group's counts sum to 64, and in every group one request holds exactly 48 pages. `text_len`: in every group one request has all 128 text tokens live.
All inputs are finite; a program needn't handle non-finite values.
Results may differ from a plain program's by a relative error of at most 0.03.
The roundings to bfloat16 on the way count: a program that leaves them out, or rounds other values in their place, can miss the bound.
Values may be sent and summed in bfloat16 or wider, within the bound.
A program may use at most 128 MiB of HBM per device.

v0:
```python
import math

import jax
import jax.numpy as jnp
from jax import lax
from jax.sharding import PartitionSpec as P

HEADS = 12
HEAD_DIM = 128
PAGE = 16
STEPS = 2


NEG_FILL = -1e30


def project(rows, weight):
    flat = jnp.dot(rows, weight, preferred_element_type=jnp.float32).astype(jnp.bfloat16)
    return flat.reshape(rows.shape[0], HEADS, HEAD_DIM)


def attend(running, query_heads, key_heads, value_heads, allowed, score_scale):
    best_score, weight_sum, value_sum = running
    scores = (
        jnp.einsum("thd,shd->ths", query_heads, key_heads, preferred_element_type=jnp.float32)
        * score_scale
    )
    scores = jnp.where(allowed[:, None, :], scores, NEG_FILL)
    new_best = jnp.maximum(best_score, jnp.max(scores, axis=2))
    shrink = jnp.exp(best_score - new_best)
    weights = jnp.exp(scores - new_best[:, :, None])
    weight_sum = weight_sum * shrink + jnp.sum(weights, axis=2)
    value_sum = value_sum * shrink[:, :, None] + jnp.einsum(
        "ths,shd->thd",
        weights.astype(jnp.bfloat16),
        value_heads,
        preferred_element_type=jnp.float32,
    )
    return (new_best, weight_sum, value_sum)


def shards(
    latent,
    incoming,
    req_pages,
    text_len,
    gate_scale,
    text_keys,
    text_values,
    w_query,
    w_key,
    w_value,
    w_out,
):
    tok_rows, channels = latent.shape
    head_count = HEADS
    head_width = HEAD_DIM
    out_slots = incoming.shape[1]
    req_count = text_keys.shape[1]
    txt_rows = text_keys.shape[2]
    keep_rows = tok_rows - out_slots * PAGE
    query_full, key_full, value_full = (
        lax.all_gather(w_query, "grp", axis=0, tiled=True),
        lax.all_gather(w_key, "grp", axis=0, tiled=True),
        lax.all_gather(w_value, "grp", axis=0, tiled=True),
    )
    arrived = lax.all_gather(latent[keep_rows:], "grp", axis=0, tiled=True)
    arrived_pages = arrived.reshape(-1, PAGE, channels)
    picked = arrived_pages[incoming[0]].reshape(out_slots * PAGE, channels)
    hidden = jnp.concatenate([latent[:keep_rows], picked], axis=0)
    route_all = lax.all_gather(incoming, "grp", axis=1, tiled=True)
    page_ends = jnp.cumsum(req_pages[0]) * PAGE

    def segment_of(positions):
        return jnp.sum((positions[:, None] >= page_ends[None, :]).astype(jnp.int32), axis=1)

    first_row = lax.axis_index("patch") * tok_rows
    query_seg = segment_of(first_row + jnp.arange(tok_rows, dtype=jnp.int32))
    score_scale = 1.0 / math.sqrt(head_width)
    owner_mask = query_seg[:, None] == jnp.arange(req_count, dtype=jnp.int32)[None, :]
    live_text = jnp.arange(txt_rows, dtype=jnp.int32)[None, :] < text_len[0][:, None]
    text_allowed = (owner_mask[:, :, None] & live_text[None]).reshape(
        tok_rows, req_count * txt_rows
    )
    keys_text = text_keys[0].reshape(req_count * txt_rows, head_count, head_width)
    values_text = text_values[0].reshape(req_count * txt_rows, head_count, head_width)
    gate_rows = jnp.sum(jnp.where(owner_mask[:, :, None], gate_scale[0][None], 0.0), axis=1)

    def visit(running, query_heads, key_heads, value_heads):
        piece_rows = key_heads.shape[0]
        key_seg = segment_of(jnp.arange(piece_rows, dtype=jnp.int32))
        allowed = query_seg[:, None] == key_seg[None, :]
        return attend(running, query_heads, key_heads, value_heads, allowed, score_scale)

    for step_index in range(STEPS):
        query_heads = project(hidden, query_full)
        start_state = (
            jnp.full((tok_rows, head_count), NEG_FILL, jnp.float32),
            jnp.zeros((tok_rows, head_count), jnp.float32),
            jnp.zeros((tok_rows, head_count, head_width), jnp.float32),
        )
        running = attend(
            start_state, query_heads, keys_text, values_text, text_allowed, score_scale
        )
        key_rows = project(hidden, key_full).reshape(tok_rows, channels)
        value_rows = project(hidden, value_full).reshape(tok_rows, channels)

        def fold_keys(running_state, pieces, offset, query_heads=query_heads):
            piece_rows = pieces[0].shape[0]
            key_heads = pieces[0].reshape(piece_rows, head_count, head_width)
            value_heads = pieces[1].reshape(piece_rows, head_count, head_width)
            return visit(running_state, query_heads, key_heads, value_heads)

        running = fold_keys(
            running,
            (
                lax.all_gather(key_rows, "patch", axis=0, tiled=True),
                lax.all_gather(value_rows, "patch", axis=0, tiled=True),
            ),
            jnp.int32(0),
        )
        best_score, weight_sum, value_sum = running
        mixed_flat = (
            (value_sum / weight_sum[:, :, None]).astype(jnp.bfloat16).reshape(tok_rows, channels)
        )
        projected = jnp.dot(mixed_flat, w_out, preferred_element_type=jnp.float32)
        hidden = (hidden.astype(jnp.float32) + gate_rows * projected).astype(jnp.bfloat16)
    group_index = lax.axis_index("grp")
    own_slots = group_index * out_slots + jnp.arange(out_slots, dtype=jnp.int32)
    slot_of = jnp.argmax((route_all[0][None, :] == own_slots[:, None]).astype(jnp.int32), axis=1)
    returned = lax.all_gather(hidden[keep_rows:], "grp", axis=0, tiled=True).reshape(
        -1, PAGE, channels
    )
    back_rows = returned[slot_of].reshape(out_slots * PAGE, channels)
    return jnp.concatenate([hidden[:keep_rows], back_rows], axis=0)


def solution(mesh):
    in_specs = (
        P(("grp", "patch"), None),
        P("patch", "grp"),
        P("grp", None),
        P("grp", None),
        P("grp", None, None),
        P("grp", None, None, None),
        P("grp", None, None, None),
        P("grp", None),
        P("grp", None),
        P("grp", None),
        P(),
    )
    out_specs = P(("grp", "patch"), None)
    return jax.shard_map(shards, mesh=mesh, in_specs=in_specs, out_specs=out_specs, check_vma=False)
```

profile of v0, /device:TPU:1, one launch (start us, length us, event | category | flops | bytes accessed | tf_op | source)
XLA Modules:
  0.0 660.6 jit_solution(11402362535552013350)
XLA Ops:
  11.8 81.5 %all-gather.10.cloned.1.call-done = bf16[512,1536]{1,0:T(8,128)(2,1)} async-done(((bf16[16,1536]{1,0:T(8,128)(2,1)}), bf16[512,1536]{1,0:T(8,128)(2,1)}) %all-gather.10.cloned.1.call-update) | async-done | bytes 1572880 | tf_op jit(solution)/shard_map/all_gather | solution.py:67
  94.0 87.1 %all-gather.14.cloned.1.call-done = bf16[1536,1536]{1,0:T(8,128)(2,1)} async-done(((bf16[48,1536]{1,0:T(8,128)(2,1)}), bf16[1536,1536]{1,0:T(8,128)(2,1)}) %all-gather.14.cloned.1.call-update) | async-done | bytes 4718608 | tf_op jit(solution)/shard_map/all_gather | solution.py:64
  181.1 3.9 convolution_convert_fusion.4
  185.0 84.4 %all-gather.18.cloned.1.call-done = bf16[1536,1536]{1,0:T(8,128)(2,1)} async-done(((bf16[48,1536]{1,0:T(8,128)(2,1)}), bf16[1536,1536]{1,0:T(8,128)(2,1)}) %all-gather.18.cloned.1.call-update) | async-done | bytes 4718608 | tf_op jit(solution)/shard_map/all_gather | solution.py:65
  269.4 3.9 convolution_convert_fusion.3
  273.8 2.2 copy.46
  276.1 2.5 reshape_squeeze.6
  278.6 3.8 copy.49
  282.4 3.6 reshape_squeeze.7
  287.9 69.7 %all-gather.12.cloned.1.call-done = bf16[1536,1536]{1,0:T(8,128)(2,1)} async-done(((bf16[48,1536]{1,0:T(8,128)(2,1)}), bf16[1536,1536]{1,0:T(8,128)(2,1)}) %all-gather.12.cloned.1.call-update) | async-done | bytes 4718608 | tf_op jit(solution)/shard_map/all_gather | solution.py:63
  357.6 3.1 convolution_convert_fusion.5
  360.9 2.4 bitcast_reduce_fusion.1
  363.4 36.3 %all-gather.16.cloned.1.call-done = bf16[1024,1536]{1,0:T(8,128)(2,1)} async-done(((bf16[128,1536]{1,0:T(8,128)(2,1)}), bf16[1024,1536]{1,0:T(8,128)(2,1)}) %all-gather.16.cloned.1.call-update) | async-done | bytes 3145744 | tf_op jit(solution)/shard_map/all_gather | solution.py:117
  399.7 4.7 copy.50
  404.3 3.6 fusion.4
  411.5 1.9 fusion.58
  413.4 34.4 %all-gather.20.cloned.1.call-done = bf16[1024,1536]{1,0:T(8,128)(2,1)} async-done(((bf16[128,1536]{1,0:T(8,128)(2,1)}), bf16[1024,1536]{1,0:T(8,128)(2,1)}) %all-gather.20.cloned.1.call-update) | async-done | bytes 3145744 | tf_op jit(solution)/shard_map/all_gather | solution.py:118
  447.8 4.7 copy.53
  452.5 6.1 fusion.73
  459.5 3.9 convolution_convert_fusion.1
  463.5 3.9 convolution_convert_fusion
  467.4 3.1 convolution_convert_fusion.2
  470.8 2.4 bitcast_reduce_fusion
  473.2 36.8 %all-gather.22.cloned.1.call-done = bf16[1024,1536]{1,0:T(8,128)(2,1)} async-done(((bf16[128,1536]{1,0:T(8,128)(2,1)}), bf16[1024,1536]{1,0:T(8,128)(2,1)}) %all-gather.22.cloned.1.call-update) | async-done | bytes 3145744 | tf_op jit(solution)/shard_map/all_gather | solution.py:117
  510.0 3.2 copy.58
  513.2 2.8 fusion.5
  519.6 1.9 fusion.61
  521.5 36.8 %all-gather.24.cloned.1.call-done = bf16[1024,1536]{1,0:T(8,128)(2,1)} async-done(((bf16[128,1536]{1,0:T(8,128)(2,1)}), bf16[1024,1536]{1,0:T(8,128)(2,1)}) %all-gather.24.cloned.1.call-update) | async-done | bytes 3145744 | tf_op jit(solution)/shard_map/all_gather | solution.py:118
  558.3 4.8 copy.61
  563.1 6.0 fusion.79
  571.9 17.4 %all-reduce = s32[32]{0:T(128)S(1)} all-reduce(s32[32]{0:T(128)S(1)} %bitcast_dynamic-update-slice_fusion), channel_id=1, replica_groups=mesh['grp'=32,'patch'=8] {'grp'}, use_global_device_ids=true, to_apply=%add | all-reduce | flops 32 | bytes 256
  591.9 60.5 %all-gather.26.cloned.1.call-done = bf16[512,1536]{1,0:T(8,128)(2,1)} async-done(((bf16[16,1536]{1,0:T(8,128)(2,1)}), bf16[512,1536]{1,0:T(8,128)(2,1)}) %all-gather.26.cloned.1.call-update) | async-done | bytes 1572880 | tf_op jit(solution)/shard_map/all_gather | solution.py:131
  (102 shorter events, 21.2 us)
Async XLA Ops:
  6.5 86.7 %all-gather.10.cloned.1.call-start = ((), (), s32[]{:S(2)}) async-start(), calls=%async_computation | async-start | bytes 1622016 | tf_op jit(solution)/shard_map/all_gather | solution.py:67
  8.0 173.1 %all-gather.14.cloned.1.call-start = ((), (), s32[]{:S(2)}) async-start(), calls=%async_computation.2 | async-start | bytes 4866048 | tf_op jit(solution)/shard_map/all_gather | solution.py:64
  8.7 260.7 %all-gather.18.cloned.1.call-start = ((), (), s32[]{:S(2)}) async-start(), calls=%async_computation.4 | async-start | bytes 4866048 | tf_op jit(solution)/shard_map/all_gather | solution.py:65
  9.5 348.1 %all-gather.12.cloned.1.call-start = ((), (), s32[]{:S(2)}) async-start(), calls=%async_computation.1 | async-start | bytes 4866048 | tf_op jit(solution)/shard_map/all_gather | solution.py:63
  10.0 389.6 %all-gather.16.cloned.1.call-start = ((), (), s32[]{:S(2)}) async-start(), calls=%async_computation.3 | async-start | bytes 3538944 | tf_op jit(solution)/shard_map/all_gather | solution.py:117
  184.9 88.4 %copy-start.16 = (s32[1,4]{1,0:T(1,128)S(1)}, s32[1,4]{1,0:T(1,128)}, u32[]{:S(2)}) copy-start(s32[1,4]{1,0:T(1,128)} %param.13) | copy-start | bytes 52
  184.9 88.9 %copy-start.11 = (bf16[1,4,128,1536]{3,2,1,0:T(8,128)(2,1)S(1)}, bf16[1,4,128,1536]{3,2,1,0:T(8,128)(2,1)}, u32[]{:S(2)}) copy-start(bf16[1,4,128,1536]{3,2,1,0:T(8,128)(2,1)} %param.16) | copy-start | bytes 4718596
  185.0 262.9 %all-gather.20.cloned.1.call-start = ((), (), s32[]{:S(2)}) async-start(), calls=%async_computation.5 | async-start | bytes 3538944 | tf_op jit(solution)/shard_map/all_gather | solution.py:118
  273.3 236.7 %all-gather.22.cloned.1.call-start = ((), (), s32[]{:S(2)}) async-start(), calls=%async_computation.6 | async-start | bytes 3538944 | tf_op jit(solution)/shard_map/all_gather | solution.py:117
  278.6 7.5 %copy-start.14 = (f32[1,4,1536]{2,1,0:T(4,128)S(1)}, f32[1,4,1536]{2,1,0:T(4,128)}, u32[]{:S(2)}) copy-start(f32[1,4,1536]{2,1,0:T(4,128)} %param.15) | copy-start | bytes 73732
  278.6 8.7 %copy-start.15 = (s32[1,4]{1,0:T(1,128)S(1)}, s32[1,4]{1,0:T(1,128)}, u32[]{:S(2)}) copy-start(s32[1,4]{1,0:T(1,128)} %param.14) | copy-start | bytes 52
  287.6 183.1 %copy-start.9 = (pred[128,512]{1,0:T(8,128)(4,1)}, pred[128,512]{1,0:T(8,128)(4,1)S(1)}, u32[]{:S(2)}) copy-start(pred[128,512]{1,0:T(8,128)(4,1)S(1)} %bitcast_and_fusion) | copy-start | bytes 196612
  287.9 164.7 %copy-start.7 = (pred[128,1024]{0,1:T(8,128)(4,1)}, pred[128,1024]{0,1:T(8,128)(4,1)S(1)}, u32[]{:S(2)}) copy-start(pred[128,1024]{0,1:T(8,128)(4,1)S(1)} %broadcast_compare_fusion) | copy-start | bytes 393220
  404.3 3.7 copy-start.3
  408.0 2.7 copy-start.1
  408.9 2.6 copy-start.12
  447.8 10.8 %slice-start = ((s8[4718592]{0:T(1024)(128)(4,1)}), s8[524288]{0:T(1024)(128)(4,1)S(1)}, s32[]{:S(2)}) async-start(s8[4718592]{0:T(1024)(128)(4,1)} %bitcast.160), calls=%async_computation.9 | async-start | bytes 1048576
  452.5 6.1 slice-start.1
  452.5 6.1 copy-start.4
  463.4 94.9 %all-gather.24.cloned.1.call-start = ((), (), s32[]{:S(2)}) async-start(), calls=%async_computation.7 | async-start | bytes 3538944 | tf_op jit(solution)/shard_map/all_gather | solution.py:118
  467.4 185.1 %all-gather.26.cloned.1.call-start = ((), (), s32[]{:S(2)}) async-start(), calls=%async_computation.8 | async-start | bytes 1622016 | tf_op jit(solution)/shard_map/all_gather | solution.py:131
  470.8 2.4 copy-start.6
  513.2 2.8 copy-start.2
  513.2 2.8 copy-start.10
  516.0 2.7 copy-start
  516.0 1.0 copy-start.8
  517.1 2.6 copy-start.13
  521.5 41.6 %copy-start.18 = (f32[128,12,128]{0,2,1:T(8,128)S(1)}, f32[128,12,128]{0,2,1:T(8,128)}, u32[]{:S(2)}) copy-start(f32[128,12,128]{0,2,1:T(8,128)} %fusion.61) | copy-start | bytes 2359300
  558.3 10.8 %slice-start.2 = ((s8[4718592]{0:T(1024)(128)(4,1)}), s8[524288]{0:T(1024)(128)(4,1)S(1)}, s32[]{:S(2)}) async-start(s8[4718592]{0:T(1024)(128)(4,1)} %bitcast.162), calls=%async_computation.11 | async-start | bytes 1048576
  563.1 6.0 slice-start.3
  563.1 6.0 copy-start.5
  569.2 1.5 copy-start.17
Sparse Core Ops, SparseCore 0:
  10.1 83.0 all-gather.9
  96.0 85.0 all-gather.13
  183.9 85.5 all-gather.17
  272.0 85.5 all-gather.11
  359.2 40.4 all-gather.15
  401.3 46.4 all-gather.19
  463.5 46.4 all-gather.21
  511.8 46.4 all-gather.23
  570.8 81.6 all-gather.25
where the time goes:
time: 662 us; the launch traced here: 661 us
  waiting for transfers between devices  530 us (80%)
  matrix products  50.4 us (8%)
  local copies, waits for them, and re-layouts  39 us (6%)
  blocking collectives  17.4 us (3%)
  between operations  16.1 us (2%)
  other arithmetic  7.75 us (1%)
    all_gather x1, waiting for transfers between devices, shards(): lax.all_gather(w_key, 'grp', axis=0, tiled=True)  87.1 us
    all_gather x1, waiting for transfers between devices, shards(): lax.all_gather(w_value, 'grp', axis=0, tiled=True)  84.4 us
    all_gather x1, waiting for transfers between devices, shards(): arrived = lax.all_gather(latent[keep_rows:], 'grp', axis=0, tiled=True)  81.5 us
    all_gather x2, waiting for transfers between devices, shards(): lax.all_gather(key_rows, 'patch', axis=0, tiled=True)  73.2 us
    all_gather x2, waiting for transfers between devices, shards(): lax.all_gather(value_rows, 'patch', axis=0, tiled=True)  71.2 us
    all_gather x1, waiting for transfers between devices, shards(): lax.all_gather(w_query, 'grp', axis=0, tiled=True)  69.7 us
    all_gather x1, waiting for transfers between devices, shards(): lax.all_gather(hidden[keep_rows:], 'grp', axis=0, tiled=True)  60.5 us
    dot_general x6, matrix products, project(): jnp.dot(rows, weight, preferred_element_type=jnp.float32)  21.7 us
  transfers between devices with their start and end apart: 9, of which 9 were waited for; matrix products, arithmetic and copies ran while one was open for 10% of the time, Pallas kernels for 0%

commit v1 on v0

v1 whole, which is shorter than its diff:
```python
import math

import jax
import jax.numpy as jnp
from jax import lax
from jax.experimental import pallas as pl
from jax.experimental.pallas import tpu as pltpu
from jax.sharding import PartitionSpec as P

MESH = pl.DeviceIdType.MESH
HEADS = 12
DIM = 128
WIDTH = 1536
PAGE = 16
REQS = 4
TXT = 128
TOK = 128
SEQ = 1024
KEEP = TOK - PAGE
NZ = 8
WROWS = 48
KEYS = SEQ + REQS * TXT
QB = 256
NEG_FILL = -1e30
TAG = 128
F32 = jnp.float32
BF16 = jnp.bfloat16
EXP_SCALE = math.log2(math.e) / math.sqrt(DIM)

PARTS = ((0, 64), (64, 48), (112, 16))


def kernel(
    lat, inc, req_pages, text_len, gate, text_k, text_v, w_q, w_k, w_v, w_o, out,
    hid, wgt, wout, mix, keys, vals, qry, mine, fin, kid,
    pages, back, ints, pick_out, pick_in,
    local_sem, z_send, z_recv, swap_send, swap_recv, yh_send, yh_recv,
    set_send, set_recv, hg_send, hg_recv, mg_send, mg_recv, aa_send, aa_recv,
):
    g = lax.axis_index("grp")
    p = lax.axis_index("patch")
    z, c = g // 4, g % 4
    x, yl = p % 4, p // 4

    def patch_of(dx, dy):
        return ((yl + dy) % 2) * 4 + (x + dx) % 4

    right, left, other = (g, patch_of(1, 0)), (g, patch_of(3, 0)), (g, patch_of(0, 1))
    up, down = ((g + 4) % 32, p), ((g + 28) % 32, p)
    core_g = (g // 2) * 2 + 1 - g % 2
    yhi_g = z * 4 + (c + 2) % 4
    core, yhi = (core_g, p), (yhi_g, p)

    def set_peer(j):
        return z * 4 + (c + j) % 4

    def zdev(dz, cc):
        return ((z + dz) % NZ) * 4 + cc

    head_a = p
    head_b = 8 + p // 2
    col_a = pl.ds(pl.multiple_of(head_a * DIM, DIM), DIM)
    col_b = pl.ds(pl.multiple_of(head_b * DIM, DIM), DIM)

    def wrows(gg):
        return wgt.at[pl.ds(pl.multiple_of(gg * WROWS, 16), WROWS), :]

    loads = []
    my_rows = pl.ds(pl.multiple_of(g * WROWS, 16), WROWS)
    for n, w in enumerate((w_q, w_k, w_v)):
        for m, col in enumerate((col_a, col_b)):
            loads.append(pltpu.make_async_copy(
                w.at[:, col], wgt.at[my_rows, pl.ds((2 * n + m) * DIM, DIM)], local_sem.at[2 * n + m]))
    text_loads = []
    for n, (src, dst) in enumerate(((text_k, keys), (text_v, vals))):
        for m, col in enumerate((col_a, col_b)):
            text_loads.append(pltpu.make_async_copy(
                src.at[:, col], dst.at[m, pl.ds(SEQ, REQS * TXT), :], local_sem.at[6 + 2 * n + m]))
    my_hid = pl.ds(pl.multiple_of(p * TOK, TOK), KEEP)
    text_loads.append(pltpu.make_async_copy(lat.at[pl.ds(0, KEEP), :], hid.at[my_hid, :], local_sem.at[10]))
    wout_load = pltpu.make_async_copy(w_o, wout, local_sem.at[11])
    page_load = pltpu.make_async_copy(lat.at[pl.ds(KEEP, PAGE), :], pages.at[z], local_sem.at[12])
    for load in loads:
        load.start()
    page_load.start()
    ints[g] = jnp.full((8, 128), inc[0, 0], jnp.int32)

    barrier = pltpu.get_barrier_semaphore()
    greeted = [up, down] + [(set_peer(j), p) for j in (1, 2, 3)]
    greeted += [(g, patch_of(dx, dy)) for dy in (0, 1) for dx in range(4) if (dx, dy) != (0, 0)]
    for peer in greeted:
        pl.semaphore_signal(barrier, inc=1, device_id=peer, device_id_type=MESH)
    pl.semaphore_wait(barrier, len(greeted))

    pending = []

    def remote(src, dst, send, recv, dev):
        return pltpu.make_async_remote_copy(
            src_ref=src, dst_ref=dst, send_sem=send, recv_sem=recv, device_id=dev, device_id_type=MESH)

    def go(*args):
        copy = remote(*args)
        copy.start()
        pending.append(copy)

    Z_FROM = (-1, -2, -3, 1, 2, 3, 4)

    def z_copy(item, at, slot, dz, dev):
        return remote(at(dz), at(dz), z_send.at[item, slot], z_recv.at[item, slot], dev)

    def z_go(item, at, slot, dz, dev):
        copy = z_copy(item, at, slot, dz, dev)
        copy.start()
        pending.append(copy)

    def z_wait(item, at, slot):
        z_copy(item, at, slot, Z_FROM[slot], up).wait_recv()

    def z_first(item, at):
        z_go(item, at, 0, 0, up)
        z_go(item, at, 3, 0, down)

    def z_step(item, at, step, last_up):
        if step == 4:
            z_wait(item, at, 6)
            return
        z_wait(item, at, step - 1)
        if step < 3:
            z_go(item, at, step, -step, up)
        elif last_up:
            z_go(item, at, 6, -3, up)
        z_wait(item, at, 2 + step)
        if step < 3:
            z_go(item, at, 3 + step, step, down)
        elif not last_up:
            z_go(item, at, 6, 3, down)

    def page_at(dz):
        return pages.at[(z + dz) % NZ]

    def back_at(dz):
        return back.at[(z + dz) % NZ]

    def own_w(dz):
        return wrows(zdev(dz, c))

    def yhi_w(dz):
        return wrows(zdev(dz, (c + 2) % 4))

    def swap(item, dz):
        cc = (c + 2 * item) % 4
        ref = wrows(zdev(dz, cc))
        go(ref, ref, swap_send.at[item, dz % NZ], swap_recv.at[item, dz % NZ], core)

    def swap_wait(item, dz):
        other_c = (c // 2) * 2 + 1 - c % 2
        ref = wrows(zdev(dz, (other_c + 2 * item) % 4))
        remote(ref, ref, swap_send.at[item, dz % NZ], swap_recv.at[item, dz % NZ], core).wait_recv()

    G_FROM = ((3, 0), (1, 0), (0, 1), (2, 0), (3, 1), (1, 1), (2, 1))

    class Gather:
        def __init__(self, send, recv, at):
            self.send, self.recv, self.at = send, recv, at

        def copy(self, k, slot, ps, dev, src=None):
            ref = self.at(k, ps)
            return remote(ref if src is None else src, ref, self.send.at[k, slot], self.recv.at[k, slot], dev)

        def go(self, k, slot, ps, dev, src=None):
            copy = self.copy(k, slot, ps, dev, src)
            copy.start()

        def first(self, k, src=None):
            self.go(k, 0, p, right, src)
            self.go(k, 1, p, left, src)
            self.go(k, 2, p, other, src)

        def wait(self, k, slot):
            self.copy(k, slot, patch_of(*G_FROM[slot]), other).wait_recv()

        def second(self, k, far_right):
            self.wait(k, 0)
            if far_right is True:
                self.go(k, 3, patch_of(3, 0), right)
            self.wait(k, 1)
            if far_right is False:
                self.go(k, 3, patch_of(1, 0), left)
            if far_right is not True and far_right is not False:
                @pl.when(far_right)
                def _():
                    self.go(k, 3, patch_of(3, 0), right)

                @pl.when(jnp.logical_not(far_right))
                def _():
                    self.go(k, 3, patch_of(1, 0), left)
            self.wait(k, 2)
            self.go(k, 4, patch_of(0, 1), right)
            self.go(k, 5, patch_of(0, 1), left)

        def third(self, k):
            self.wait(k, 3)
            self.go(k, 6, patch_of(2, 0), other)

        def last(self, k):
            self.wait(k, 4)
            self.wait(k, 5)
            self.wait(k, 6)

        def drain(self, k):
            for slot in range(7):
                self.copy(k, slot, p, other).wait_send()

    def hid_at(k, ps):
        first, rows = PARTS[k]
        return hid.at[pl.ds(pl.multiple_of(ps * TOK + first, 16), rows), :]

    hg = Gather(hg_send, hg_recv, hid_at)

    page_load.wait()
    z_first(0, page_at)
    for j in (1, 2, 3):
        go(ints.at[g], ints.at[g], set_send.at[0, j - 1], set_recv.at[0, j - 1], (set_peer(j), p))
    hg.first(0, lat.at[pl.ds(0, 64), :])
    hg.first(1, lat.at[pl.ds(64, 48), :])
    for load in loads:
        load.wait()
    go(wrows(g), wrows(g), yh_send, yh_recv, yhi)
    z_first(1, own_w)
    swap(0, 0)
    for load in text_loads:
        load.start()
    wout_load.start()

    ends = []
    total = jnp.int32(0)
    for r in range(REQS):
        total = total + req_pages[0, r] * PAGE
        ends.append(total)

    def segment(pos):
        seg = jnp.zeros(pos.shape, jnp.int32)
        for r in range(REQS):
            seg = seg + (pos >= ends[r]).astype(jnp.int32)
        return seg

    kid[:, 0:SEQ] = segment(lax.broadcasted_iota(jnp.int32, (8, SEQ), 1))
    for r in range(REQS):
        j = lax.broadcasted_iota(jnp.int32, (8, TXT), 1)
        kid[:, SEQ + r * TXT:SEQ + (r + 1) * TXT] = jnp.where(j < text_len[0, r], r, -1)

    z_step(0, page_at, 1, True)
    remote(wrows(yhi_g), wrows(yhi_g), yh_send, yh_recv, yhi).wait_recv()
    z_first(2, yhi_w)
    swap(1, 0)
    z_step(0, page_at, 2, True)
    z_step(0, page_at, 3, True)
    z_step(1, own_w, 1, True)
    z_step(0, page_at, 4, True)

    def route(ring, kind, want):
        own = None
        for j in (1, 2, 3, 0):
            acc = jnp.zeros((PAGE, WIDTH), F32)
            for zz in range(NZ):
                page = ring[zz, :, 0:WIDTH].astype(F32)
                acc = acc + jnp.where(want(zz, j), page, 0.0)
            if j:
                pick_out[kind, j - 1] = acc.astype(BF16)
                go(pick_out.at[kind, j - 1], pick_in.at[kind, j - 1],
                   set_send.at[1 + kind, j - 1], set_recv.at[1 + kind, j - 1], (set_peer(j), p))
            else:
                own = acc
        for j in (1, 2, 3):
            remote(pick_out.at[kind, j - 1], pick_in.at[kind, j - 1],
                   set_send.at[1 + kind, j - 1], set_recv.at[1 + kind, j - 1], core).wait_recv()
            own = own + pick_in[kind, j - 1].astype(F32)
        return own.astype(BF16)

    for j in (1, 2, 3):
        src = set_peer(4 - j)
        remote(ints.at[src], ints.at[src], set_send.at[0, j - 1], set_recv.at[0, j - 1], core).wait_recv()

    def want_in(zz, j):
        return ints[set_peer(j), 0:1, 0:1] == zz * 4 + c

    taken = route(pages, 0, want_in)
    hid[pl.ds(pl.multiple_of(p * TOK + KEEP, 16), PAGE), :] = taken
    hg.first(2)

    z_step(2, yhi_w, 1, False)
    z_step(1, own_w, 2, True)
    z_step(2, yhi_w, 2, False)
    for item in (0, 1):
        for dz in (-1, 1):
            swap(item, dz)
    hg.second(0, True)
    hg.second(1, False)
    z_step(1, own_w, 3, True)
    z_step(2, yhi_w, 3, False)
    for item in (0, 1):
        for dz in (-2, 2, -3, 3):
            swap(item, dz)
    hg.second(2, True)
    z_step(1, own_w, 4, True)
    z_step(2, yhi_w, 4, False)
    for item in (0, 1):
        swap(item, 4)
    hg.third(0)
    hg.third(1)
    hg.third(2)
    for item in (0, 1):
        for dz in range(NZ):
            swap_wait(item, dz)
    for k in range(3):
        hg.last(k)
    for load in text_loads:
        load.wait()
    wout_load.wait()

    def rows_of(start, size=QB):
        return pl.ds(pl.multiple_of(start, 128), size)

    def project(t):
        rows = rows_of(t * QB)
        y = jnp.dot(hid[rows, :], wgt[...], preferred_element_type=F32).astype(BF16)
        for m in range(2):
            qry[m, rows, :] = y[:, m * DIM:(m + 1) * DIM]
            keys[m, rows, :] = y[:, (2 + m) * DIM:(3 + m) * DIM]
            vals[m, rows, :] = y[:, (4 + m) * DIM:(5 + m) * DIM]

    def attend(m, tok):
        q = qry[m, rows_of(tok), :]
        s = lax.dot_general(q, keys[m], (((1,), (1,)), ((), ())), preferred_element_type=F32)
        qseg = segment(tok + lax.broadcasted_iota(jnp.int32, (QB, 1), 0))
        s = jnp.where(qseg == kid[0:1, :], s, NEG_FILL)
        best = jnp.max(s, axis=1, keepdims=True)
        w = jnp.exp2((s - best) * EXP_SCALE)
        total_w = jnp.sum(w, axis=1, keepdims=True)
        o = jnp.dot(w.astype(BF16), vals[m], preferred_element_type=F32)
        return (o / total_w).astype(BF16)

    def gated(rows, start, heads):
        size = heads[0].shape[0]
        seg = segment(start + lax.broadcasted_iota(jnp.int32, (size, 1), 0))
        a = jnp.concatenate(heads, axis=1)

        def tile(n, carry):
            cols = pl.ds(pl.multiple_of(n * 512, 512), 512)
            proj = jnp.dot(a, wout[:, cols], preferred_element_type=F32)
            scale = gate[3:4, cols]
            for r in (2, 1, 0):
                scale = jnp.where(seg == r, gate[r:r + 1, cols], scale)
            hid[rows, cols] = (hid[rows, cols].astype(F32) + scale * proj).astype(BF16)
            return carry

        lax.fori_loop(0, 3, tile, 0)

    def item_of(k, ps):
        is_b = jnp.logical_or(k == 1, k == 3)
        tok_a = jnp.where(k == 0, 0, jnp.where(k == 2, 2, jnp.where(k == 4, 1, 3)))
        tok_b = (ps % 2) * 2 + jnp.where(k == 1, 0, 1)
        head = jnp.where(is_b, 8 + ps // 2, ps)
        return is_b.astype(jnp.int32), head, jnp.where(is_b, tok_b, tok_a) * QB

    def mix_at(k, ps):
        _, head, tok = item_of(k, ps)
        return mix.at[head, rows_of(tok), :]

    mg = Gather(mg_send, mg_recv, mix_at)

    def do_project(t, carry):
        project(t)
        return carry

    lax.fori_loop(0, SEQ // QB, do_project, 0)

    def step_one(k, carry):
        m, head, tok = item_of(k, p)
        mix[head, rows_of(tok), :] = attend(m, tok)
        mg.first(k)

        @pl.when(k >= 1)
        def _():
            mg.second(k - 1, (k - 1) % 2 == 0)

        @pl.when(k >= 2)
        def _():
            mg.third(k - 2)
        return carry

    lax.fori_loop(0, 6, step_one, 0)

    def widen(t):
        rows = rows_of(t * QB)
        gated(rows, t * QB, [mix[h, rows, :] for h in range(HEADS)])
        project(t)

    for k in range(3):
        hg.drain(k)
    mg.second(5, False)
    mg.third(4)
    mg.last(0)
    mg.last(1)
    widen(0)
    mg.third(5)
    mg.last(2)
    widen(2)
    mg.last(3)
    mg.last(4)
    widen(1)
    mg.last(5)
    widen(3)

    def piece(k, half, sent):
        m, head, tok = item_of(k, p)
        d = tok // TOK + half
        src = mine.at[k, pl.ds(half * TOK, TOK), :]

        if not sent:
            @pl.when(d == p)
            def _():
                pltpu.make_async_copy(src, fin.at[head], aa_recv.at[head]).start()

        @pl.when(d != p)
        def _():
            copy = remote(src, fin.at[head], aa_send.at[k, half], aa_recv.at[head], (g, d))
            if sent:
                copy.wait_send()
            else:
                copy.start()

    def step_two(k, carry):
        m, head, tok = item_of(k, p)
        mine[k] = attend(m, tok)
        for half in (0, 1):
            piece(k, half, False)
        return carry

    lax.fori_loop(0, 6, step_two, 0)

    def take_head(h, carry):
        remote(fin.at[h], fin.at[h], aa_send.at[0, 0], aa_recv.at[h], other).wait_recv()
        return carry

    lax.fori_loop(0, HEADS, take_head, 0)
    own_rows = rows_of(p * TOK, TOK)
    gated(own_rows, p * TOK, [fin[h] for h in range(HEADS)])
    back[z, :, 0:WIDTH] = hid[pl.ds(pl.multiple_of(p * TOK + KEEP, 16), PAGE), :]
    back[z, :, WIDTH:] = jnp.full((PAGE, TAG), inc[0, 0], jnp.int32).astype(F32).astype(BF16)
    z_first(3, back_at)
    out[0:KEEP, :] = hid[pl.ds(pl.multiple_of(p * TOK, 16), KEEP), :]
    for step in (1, 2, 3, 4):
        z_step(3, back_at, step, True)

    def want_back(zz, j):
        tag = back[zz, :, WIDTH:WIDTH + 1].astype(F32)
        return tag == set_peer(j).astype(F32)

    out[KEEP:TOK, :] = route(back, 1, want_back)

    for copy in pending:
        copy.wait_send()

    def drain(k, carry):
        mg.drain(k)
        for half in (0, 1):
            piece(k, half, True)
        return carry

    lax.fori_loop(0, 6, drain, 0)


def shards(latent, incoming, req_pages, text_len, gate_scale, text_keys, text_values, w_query, w_key, w_value, w_out):
    vm = pl.BlockSpec(memory_space=pltpu.VMEM)
    sm = pl.BlockSpec(memory_space=pltpu.SMEM)
    hb = pl.BlockSpec(memory_space=pl.ANY)
    dma = pltpu.SemaphoreType.DMA
    return pl.pallas_call(
        kernel,
        out_shape=jax.ShapeDtypeStruct((TOK, WIDTH), BF16),
        in_specs=[hb, sm, sm, sm, vm, hb, hb, hb, hb, hb, hb],
        out_specs=vm,
        scratch_shapes=[
            pltpu.VMEM((SEQ, WIDTH), BF16),
            pltpu.VMEM((WIDTH, 6 * DIM), BF16),
            pltpu.VMEM((WIDTH, WIDTH), BF16),
            pltpu.VMEM((HEADS, SEQ, DIM), BF16),
            pltpu.VMEM((2, KEYS, DIM), BF16),
            pltpu.VMEM((2, KEYS, DIM), BF16),
            pltpu.VMEM((2, SEQ, DIM), BF16),
            pltpu.VMEM((6, QB, DIM), BF16),
            pltpu.VMEM((HEADS, TOK, DIM), BF16),
            pltpu.VMEM((8, KEYS), jnp.int32),
            pltpu.VMEM((NZ, PAGE, WIDTH), BF16),
            pltpu.VMEM((NZ, PAGE, WIDTH + TAG), BF16),
            pltpu.VMEM((32, 8, 128), jnp.int32),
            pltpu.VMEM((2, 3, PAGE, WIDTH), BF16),
            pltpu.VMEM((2, 3, PAGE, WIDTH), BF16),
            dma((13,)),
            dma((4, 7)), dma((4, 7)),
            dma((2, NZ)), dma((2, NZ)),
            dma, dma,
            dma((3, 3)), dma((3, 3)),
            dma((3, 7)), dma((3, 7)),
            dma((6, 7)), dma((6, 7)),
            dma((6, 2)), dma((HEADS,)),
        ],
        compiler_params=pltpu.CompilerParams(
            collective_id=0, has_side_effects=True, vmem_limit_bytes=50 * 1024 * 1024),
        cost_estimate=pl.CostEstimate(flops=14_000_000_000, bytes_accessed=10_000_000, transcendentals=5_000_000),
    )(
        latent, incoming, req_pages, text_len, gate_scale[0],
        text_keys.reshape(REQS * TXT, WIDTH), text_values.reshape(REQS * TXT, WIDTH),
        w_query, w_key, w_value, w_out,
    )


def solution(mesh):
    in_specs = (
        P(("grp", "patch"), None),
        P("patch", "grp"),
        P("grp", None),
        P("grp", None),
        P("grp", None, None),
        P("grp", None, None, None),
        P("grp", None, None, None),
        P("grp", None),
        P("grp", None),
        P("grp", None),
        P(),
    )
    return jax.shard_map(
        shards, mesh=mesh, in_specs=in_specs, out_specs=P(("grp", "patch"), None), check_vma=False)
```

time: 662 us -> 129 us (0.19)
  waiting for transfers between devices: 530 us -> 0 us
  Pallas kernels: 0 us -> 119 us
  matrix products: 50.4 us -> 0 us
  local copies, waits for them, and re-layouts: 39 us -> 7.92 us
  blocking collectives: 17.4 us -> 0 us
  between operations: 16.1 us -> 0.68 us
  other arithmetic: 7.75 us -> 0 us
    all_gather x9 -> x0, waiting for transfers between devices: 528 us -> none  [the longest x1 87.1 us: shards(): lax.all_gather(w_key, 'grp', axis=0, tiled=True)]
    pallas_call x0 -> x1, Pallas kernels: none -> 119 us  [shards(): pl.pallas_call(kernel, out_shape=jax.ShapeDtypeStruct((TOK, WIDTH), BF16)...]
    dot_general x16 -> x0, matrix products: 50.4 us -> none  [the longest x6 21.7 us: project(): jnp.dot(rows, weight, preferred_element_type=jnp.float32)]
    unnamed x1 -> x0, blocking collectives: 17.4 us -> none
    all_gather x4 -> x0, local copies, waits for them, and re-layouts: 17.4 us -> none  [the longest x2 9.52 us: shards(): lax.all_gather(value_rows, 'patch', axis=0, tiled=True)]
  transfers between devices with their start and end apart: 9 -> 0, of which waited for: 9 -> 0; matrix products, arithmetic and copies ran while one was open for 10% -> 0% of each run, Pallas kernels for 0% -> 0%
where the time goes in v1:
time: 129 us; the launch traced here: 128 us
  Pallas kernels  119 us (92%)
  local copies, waits for them, and re-layouts  7.92 us (6%)
    pallas_call x1, Pallas kernels, shards(): pl.pallas_call(kernel, out_shape=jax.ShapeDtypeStruct((TOK, WIDTH), BF16)...  119 us
    unnamed x17, local copies, waits for them, and re-layouts  7.92 us

profile of v1, /device:TPU:1, one launch (start us, length us, event | category | flops | bytes accessed | tf_op | source)
XLA Modules:
  0.0 127.9 jit_solution(4237335379573578071)
XLA Ops:
  0.7 0.0 copy-start
  0.7 1.4 %copy-done = bf16[1,4,128,1536]{3,2,1,0:T(8,128)(2,1)S(1)} copy-done((bf16[1,4,128,1536]{3,2,1,0:T(8,128)(2,1)S(1)}, bf16[1,4,128,1536]{3,2,1,0:T(8,128)(2,1)}, u32[]{:S(2)}) %copy-start) | copy-done | bytes 1572888
  2.1 0.0 copy-start.1
  2.1 1.0 copy-done.1
  3.1 0.0 copy-start.2
  3.1 0.9 copy-done.2
  4.0 0.0 copy-start.3
  4.0 0.9 copy-done.3
  4.9 0.0 copy-start.4
  4.9 0.9 copy-done.4
  5.8 0.0 copy-start.5
  5.8 0.7 copy-done.5
  6.5 0.0 copy-start.6
  6.5 0.7 copy-done.6
  7.2 0.0 copy-start.7
  7.2 0.7 copy-done.7
  7.8 119.3 %shard_map.109 = bf16[128,1536]{1,0:T(8,128)(2,1)S(1)} custom-call(bf16[128,1536]{1,0:T(8,128)(2,1)S(1)} %copy-done.1, s32[1,1]{1,0:T(1,128)S(6)} %copy.13.inc, s32[1,4]{1,0:T(1,128)S(1)} %copy-done.6, s32[1,4]{1,0:T(1,128)S(1)} %copy-done.7, f32[4,1536]{1,0:T(4,128)S(1)} %bitcast.4, bf16[512,1536]{1,0:T(8,128)(2,1)S(1)} %bitcast.3, ...), custom_call_target="tpu_custom_call" | custom-call | flops 14000000000 | bytes 10000000 | tf_op jit(solution)/shard_map/pallas_call | solution.py:479
  127.2 0.7 copy.14
Async XLA Ops:
  0.7 1.4 %copy-start = (bf16[1,4,128,1536]{3,2,1,0:T(8,128)(2,1)S(1)}, bf16[1,4,128,1536]{3,2,1,0:T(8,128)(2,1)}, u32[]{:S(2)}) copy-start(bf16[1,4,128,1536]{3,2,1,0:T(8,128)(2,1)} %param.16) | copy-start | bytes 4718596
  2.1 1.0 copy-start.1
  3.1 0.9 copy-start.2
  4.0 0.9 copy-start.3
  4.9 0.9 copy-start.4
  5.8 0.7 copy-start.5
  6.5 0.7 copy-start.6
  7.2 0.7 copy-start.7

commit v2 on v1

v2 whole, which is shorter than its diff:
```python
import math

import jax
import jax.numpy as jnp
from jax import lax
from jax.experimental import pallas as pl
from jax.experimental.pallas import tpu as pltpu
from jax.sharding import PartitionSpec as P

MESH = pl.DeviceIdType.MESH
HEADS = 12
DIM = 128
WIDTH = 1536
PAGE = 16
REQS = 4
TXT = 128
TOK = 128
SEQ = 1024
KEEP = TOK - PAGE
NZ = 8
WROWS = 48
KEYS = SEQ + REQS * TXT
QB = 256
NEG_FILL = -1e30
TAG = 128
F32 = jnp.float32
BF16 = jnp.bfloat16
EXP_SCALE = math.log2(math.e) / math.sqrt(DIM)

PARTS = ((0, 64), (64, 48), (112, 16))


def kernel(
    lat, inc_h, req_pages_h, text_len_h, gate_h, text_k, text_v, w_q, w_k, w_v, w_o, out,
    hid, home, wgt, wout, mix, keys, vals, qry, mine, fin, kid,
    pages, back, ints, pick_out, pick_in, info, gate_w,
    inc, req_pages, text_len, gate, local_sem, z_send, z_recv, swap_send, swap_recv, yh_send, yh_recv,
    int_send, int_recv, set_send, set_recv, part_send, part_recv, text_send, text_recv,
    hg_send, hg_recv, mg_send, mg_recv, home_send, home_recv, aa_send, aa_recv,
):
    g = lax.axis_index("grp")
    p = lax.axis_index("patch")
    z, c = g // 4, g % 4
    yh, k = c // 2, c % 2
    x, yl = p % 4, p // 4
    same = k == yl
    apart = k != yl
    p4 = (p + 4) % 8
    core_g = g + 1 - 2 * k
    work_g = z * 4 + yh * 2 + yl

    right, left, far = (g, yl * 4 + (x + 1) % 4), (g, yl * 4 + (x + 3) % 4), (g, yl * 4 + (x + 2) % 4)
    up, down = ((g + 4) % 32, p), ((g + 28) % 32, p)
    yhi_g = z * 4 + (c + 2) % 4
    core, yhi, partner = (core_g, p), (yhi_g, p), (core_g, p4)

    def set_peer(j):
        return z * 4 + (c + j) % 4

    def zdev(dz, cc):
        return ((z + dz) % NZ) * 4 + cc

    head_a, head_b = 3 * x + 2 * k, 3 * x + 1

    def cols_of(head):
        return pl.ds(pl.multiple_of(head * DIM, DIM), DIM)

    def wrows(gg, first=0, count=3):
        return wgt.at[pl.ds(first, count), pl.ds(pl.multiple_of(gg * WROWS, 16), WROWS), :]

    loads = []
    my_rows = pl.ds(pl.multiple_of(g * WROWS, 16), WROWS)
    for n, w in enumerate((w_q, w_k, w_v)):
        for h in range(3):
            loads.append(pltpu.make_async_copy(
                w.at[:, cols_of(3 * x + h)], wgt.at[h, my_rows, pl.ds(n * DIM, DIM)], local_sem.at[3 * n + h]))
    my_hid = pl.ds(pl.multiple_of(p * TOK, TOK), KEEP)

    def text_copies(fn, heads):
        for n, (src, dst) in enumerate(((text_k, keys), (text_v, vals))):
            for m in range(2):
                fn(src.at[:, cols_of(heads[m])], dst.at[m, pl.ds(SEQ, REQS * TXT), :], 2 * n + m)

    def own_loads(fn):
        text_copies(lambda src, dst, n: fn(pltpu.make_async_copy(src, dst, local_sem.at[9 + n])), (head_a, head_b))
        fn(pltpu.make_async_copy(lat.at[pl.ds(0, KEEP), :], hid.at[my_hid, :], local_sem.at[13]))
        fn(pltpu.make_async_copy(gate_h, gate_w, local_sem.at[14]))

    wout_load = pltpu.make_async_copy(w_o, wout, local_sem.at[15])
    page_load = pltpu.make_async_copy(lat.at[pl.ds(KEEP, PAGE), :], pages.at[z], local_sem.at[16])
    small_loads = [
        pltpu.make_async_copy(src, dst, local_sem.at[17 + n])
        for n, (src, dst) in enumerate(((inc_h, inc), (req_pages_h, req_pages), (text_len_h, text_len), (gate_h, gate)))]
    page_load.start()
    for load in small_loads + loads:
        load.start()

    barrier = pltpu.get_barrier_semaphore()
    greeted = [up, down]
    plane = z * 4 + yh * 2
    for dk in range(2):
        for dp in range(8):
            if (dk, dp) != (0, 0):
                greeted.append((plane + (k + dk) % 2, (p + dp) % 8))
    other_plane = z * 4 + (1 - yh) * 2
    greeted += [(other_plane + dk, pp) for dk in range(2) for pp in (p, p4)]
    for peer in greeted:
        pl.semaphore_signal(barrier, inc=1, device_id=peer, device_id_type=MESH)
    pl.semaphore_wait(barrier, len(greeted))

    pending = []

    def remote(src, dst, send, recv, dev):
        return pltpu.make_async_remote_copy(
            src_ref=src, dst_ref=dst, send_sem=send, recv_sem=recv, device_id=dev, device_id_type=MESH)

    def go(*args):
        copy = remote(*args)
        copy.start()
        pending.append(copy)

    Z_FROM = (-1, -2, -3, 1, 2, 3, 4)

    def z_copy(item, at, slot, dz, dev):
        return remote(at(dz), at(dz), z_send.at[item, slot], z_recv.at[item, slot], dev)

    def z_go(item, at, slot, dz, dev):
        copy = z_copy(item, at, slot, dz, dev)
        copy.start()
        pending.append(copy)

    def z_wait(item, at, slot):
        z_copy(item, at, slot, Z_FROM[slot], up).wait_recv()

    def z_first(item, at):
        z_go(item, at, 0, 0, up)
        z_go(item, at, 3, 0, down)

    def z_step(item, at, step, last_up):
        if step == 4:
            z_wait(item, at, 6)
            return
        z_wait(item, at, step - 1)
        if step < 3:
            z_go(item, at, step, -step, up)
        elif last_up:
            z_go(item, at, 6, -3, up)
        z_wait(item, at, 2 + step)
        if step < 3:
            z_go(item, at, 3 + step, step, down)
        elif not last_up:
            z_go(item, at, 6, 3, down)

    def page_at(dz):
        return pages.at[(z + dz) % NZ]

    def back_at(dz):
        return back.at[(z + dz) % NZ]

    def own_w(dz):
        return wrows(zdev(dz, c))

    def yhi_w(dz):
        return wrows(zdev(dz, (c + 2) % 4))

    def swap(item, dz):
        ref = wrows(zdev(dz, (c + 2 * item) % 4), 1 - k, 2)
        go(ref, ref, swap_send.at[item, dz % NZ], swap_recv.at[item, dz % NZ], core)

    def swap_wait(item, dz):
        other_c = 2 * yh + 1 - k
        ref = wrows(zdev(dz, (other_c + 2 * item) % 4), k, 2)
        remote(ref, ref, swap_send.at[item, dz % NZ], swap_recv.at[item, dz % NZ], core).wait_recv()

    X_FROM = (3, 1, 2, 0, 3, 1, 2)

    class Gather:
        def __init__(self, send, recv, at):
            self.send, self.recv, self.at = send, recv, at

        def copy(self, n, slot, kk, dx, dev, src=None):
            ref = self.at(n, kk, (x + dx) % 4)
            return remote(ref if src is None else src, ref, self.send.at[n, slot], self.recv.at[n, slot], dev)

        def go(self, n, slot, dx, dev, src=None):
            self.copy(n, slot, k, dx, dev, src).start()

        def first(self, n, src=None):
            self.go(n, 0, 0, right, src)
            self.go(n, 1, 0, left, src)
            self.go(n, 3, 0, core, src)

        def direct(self, n):
            self.first(n)
            self.go(n, 2, 0, far)

        def wait(self, n, slot):
            self.copy(n, slot, k if slot < 3 else 1 - k, X_FROM[slot], core).wait_recv()

        def second(self, n, far_right):
            self.wait(n, 0)
            if far_right is True:
                self.go(n, 2, 3, right)
            self.go(n, 4, 3, core)
            self.wait(n, 1)
            if far_right is False:
                self.go(n, 2, 1, left)
            if far_right is not None and not isinstance(far_right, bool):
                @pl.when(far_right)
                def _():
                    self.go(n, 2, 3, right)

                @pl.when(jnp.logical_not(far_right))
                def _():
                    self.go(n, 2, 1, left)
            self.go(n, 5, 1, core)

        def third(self, n):
            self.wait(n, 2)
            self.go(n, 6, 2, core)

        def last(self, n):
            for slot in (3, 4, 5, 6):
                self.wait(n, slot)

        def drain(self, n):
            for slot in range(7):
                self.copy(n, slot, k, 0, core).wait_send()

    def hid_at(n, kk, xx):
        first, rows = PARTS[n]
        return hid.at[pl.ds(pl.multiple_of((kk * 4 + xx) * TOK + first, 16), rows), :]

    hg = Gather(hg_send, hg_recv, hid_at)

    def lat_part(n):
        return lat.at[pl.ds(*PARTS[n]), :]

    def part_copy(n):
        first, rows = PARTS[n]
        dst = hid.at[pl.ds(pl.multiple_of(p * TOK + first, 16), rows), :]
        return remote(lat_part(n), dst, part_send.at[n], part_recv.at[n], partner)

    def part_taken(n):
        return remote(lat_part(n), hid_at(n, k, x), part_send.at[n], part_recv.at[n], partner)

    page_load.wait()
    z_first(0, page_at)

    @pl.when(same)
    def _():
        for n in range(2):
            hg.first(n, lat_part(n))

    @pl.when(apart)
    def _():
        for n in range(2):
            part_copy(n).start()

    for load in loads:
        load.wait()
    z_first(1, own_w)
    go(wrows(g), wrows(g), yh_send, yh_recv, yhi)
    for load in small_loads:
        load.wait()
    ints[g] = jnp.full((8, 128), inc[0, 0], jnp.int32)
    for j in (1, 2, 3):
        go(ints.at[g], ints.at[g], int_send.at[j - 1], int_recv.at[j - 1], (set_peer(j), p))
    swap(0, 0)

    own_ends = []
    total = jnp.int32(0)
    for r in range(REQS):
        total = total + req_pages[0, r] * PAGE
        own_ends.append(total)

    def shared_copies(fn):
        fn(remote(info, info, text_send.at[4], text_recv.at[4], core))
        fn(remote(gate_h, gate_w, text_send.at[5], text_recv.at[5], core))
        text_copies(lambda src, dst, n: fn(remote(src, dst, text_send.at[n], text_recv.at[n], core)),
                    (3 * x + 2 - 2 * k, head_b))

    @pl.when(same)
    def _():
        for r in range(REQS):
            info[r] = jnp.full((8, 128), own_ends[r], jnp.int32)
            info[REQS + r] = jnp.full((8, 128), text_len[0, r], jnp.int32)
        own_loads(lambda copy: copy.start())
        shared_copies(lambda copy: copy.start())

    wout_load.start()

    def route_to(kind, cc):
        if kind:
            return (z * 4 + cc, p), c == cc
        here = yl == cc % 2
        return (z * 4 + jnp.where(here, cc, cc + 1 - 2 * (cc % 2)), jnp.where(here, p, p4)), jnp.logical_and(c == cc, same)

    def route_copy(kind, cc, slot, dev):
        return remote(pick_out.at[kind, cc], pick_in.at[kind, slot], set_send.at[kind, cc], set_recv.at[kind, slot], dev)

    def route_send(ring, kind, want):
        for cc in range(4):
            acc = jnp.zeros((PAGE, WIDTH), F32)
            for zz in range(NZ):
                acc = acc + jnp.where(want(zz, cc), ring[zz, :, 0:WIDTH].astype(F32), 0.0)
            dev, here = route_to(kind, cc)
            pick_out[kind, cc] = acc.astype(BF16)

            @pl.when(jnp.logical_not(here))
            def _():
                route_copy(kind, cc, c, dev).start()

            @pl.when(here)
            def _():
                pick_in[kind, cc] = acc.astype(BF16)

    def route_take(kind):
        for cc in range(4):
            @pl.when(jnp.logical_not(jnp.logical_and(c == cc, same) if not kind else c == cc))
            def _():
                route_copy(kind, cc, cc, core).wait_recv()
        return sum(pick_in[kind, cc].astype(F32) for cc in range(4)).astype(BF16)

    def route_drain(kind):
        for cc in range(4):
            dev, here = route_to(kind, cc)

            @pl.when(jnp.logical_not(here))
            def _():
                route_copy(kind, cc, c, dev).wait_send()

    def want_in(zz, cc):
        return ints[z * 4 + cc, 0:1, 0:1] == zz * 4 + c

    z_step(0, page_at, 1, True)
    z_step(1, own_w, 1, True)
    remote(wrows(yhi_g), wrows(yhi_g), yh_send, yh_recv, yhi).wait_recv()
    z_first(2, yhi_w)
    swap(1, 0)

    @pl.when(apart)
    def _():
        for n in range(2):
            part_taken(n).wait_recv()
            hg.first(n)

    z_step(0, page_at, 2, True)
    for dz in (-1, 1):
        swap(0, dz)
    z_step(1, own_w, 2, True)
    z_step(2, yhi_w, 1, False)
    z_step(0, page_at, 3, True)
    for dz in (-2, 2):
        swap(0, dz)
    for dz in (-1, 1):
        swap(1, dz)
    hg.second(0, True)
    hg.second(1, False)
    z_step(1, own_w, 3, True)
    z_step(2, yhi_w, 2, False)
    z_step(0, page_at, 4, True)
    for j in (1, 2, 3):
        src = set_peer(4 - j)
        remote(ints.at[src], ints.at[src], int_send.at[j - 1], int_recv.at[j - 1], core).wait_recv()
    route_send(pages, 0, want_in)
    z_step(2, yhi_w, 3, False)
    for dz in (-3, 3):
        swap(0, dz)
    for dz in (-2, 2, -3, 3):
        swap(1, dz)
    hid[pl.ds(pl.multiple_of((k * 4 + x) * TOK + KEEP, 16), PAGE), :] = route_take(0)
    hg.direct(2)
    hg.third(0)
    hg.third(1)
    z_step(1, own_w, 4, True)
    swap(0, 4)
    z_step(2, yhi_w, 4, False)
    swap(1, 4)

    @pl.when(same)
    def _():
        own_loads(lambda copy: copy.wait())

    @pl.when(apart)
    def _():
        shared_copies(lambda copy: copy.wait_recv())

    ends = [info[r, 0:1, 0:1] for r in range(REQS)]

    def segment(pos, bounds):
        seg = jnp.zeros(pos.shape, jnp.int32)
        for r in range(REQS):
            seg = seg + (pos >= bounds[r]).astype(jnp.int32)
        return seg

    kid[:, 0:SEQ] = segment(lax.broadcasted_iota(jnp.int32, (8, SEQ), 1), ends)
    for r in range(REQS):
        j = lax.broadcasted_iota(jnp.int32, (8, TXT), 1)
        kid[:, SEQ + r * TXT:SEQ + (r + 1) * TXT] = jnp.where(j < info[REQS + r, 0:1, 0:1], r, -1)

    wout_load.wait()
    hg.second(2, None)
    hg.third(2)
    for item in (0, 1):
        for dz in range(NZ):
            swap_wait(item, dz)
    for n in range(3):
        hg.last(n)

    def rows_of(start, size=QB):
        return pl.ds(pl.multiple_of(start, 128), size)

    def project(t):
        rows = rows_of(t * QB)
        w = jnp.concatenate([wgt[2 * k], wgt[1]], axis=1)
        y = jnp.dot(hid[rows, :], w, preferred_element_type=F32).astype(BF16)
        for m in range(2):
            qry[m, rows, :] = y[:, (3 * m) * DIM:(3 * m + 1) * DIM]
            keys[m, rows, :] = y[:, (3 * m + 1) * DIM:(3 * m + 2) * DIM]
            vals[m, rows, :] = y[:, (3 * m + 2) * DIM:(3 * m + 3) * DIM]

    def attend(m, tok):
        q = qry[m, rows_of(tok), :]
        s = lax.dot_general(q, keys[m], (((1,), (1,)), ((), ())), preferred_element_type=F32)
        qseg = segment(tok + lax.broadcasted_iota(jnp.int32, (QB, 1), 0), ends)
        s = jnp.where(qseg == kid[0:1, :], s, NEG_FILL)
        best = jnp.max(s, axis=1, keepdims=True)
        w = jnp.exp2((s - best) * EXP_SCALE)
        total_w = jnp.sum(w, axis=1, keepdims=True)
        o = jnp.dot(w.astype(BF16), vals[m], preferred_element_type=F32)
        return (o / total_w).astype(BF16)

    def gated(ref, rows, start, heads, bounds, gates):
        size = heads[0].shape[0]
        seg = segment(start + lax.broadcasted_iota(jnp.int32, (size, 1), 0), bounds)
        a = jnp.concatenate(heads, axis=1)

        def tile(n, carry):
            cols = pl.ds(pl.multiple_of(n * 512, 512), 512)
            proj = jnp.dot(a, wout[:, cols], preferred_element_type=F32)
            scale = gates[3:4, cols]
            for r in (2, 1, 0):
                scale = jnp.where(seg == r, gates[r:r + 1, cols], scale)
            ref[rows, cols] = (ref[rows, cols].astype(F32) + scale * proj).astype(BF16)
            return carry

        lax.fori_loop(0, 3, tile, 0)

    def item_of(n, kk, xx):
        is_b = jnp.logical_or(n == 1, n == 3)
        tok_a = jnp.where(n == 0, 0, jnp.where(n == 2, 2, jnp.where(n == 4, 1, 3)))
        tok_b = kk * 2 + jnp.where(n == 1, 0, 1)
        head = 3 * xx + jnp.where(is_b, 1, 2 * kk)
        return is_b.astype(jnp.int32), head, jnp.where(is_b, tok_b, tok_a) * QB

    def mix_at(n, kk, xx):
        _, head, tok = item_of(n, kk, xx)
        return mix.at[head, rows_of(tok), :]

    mg = Gather(mg_send, mg_recv, mix_at)

    def do_project(t, carry):
        project(t)
        return carry

    lax.fori_loop(0, SEQ // QB, do_project, 0)

    def step_one(n, carry):
        m, head, tok = item_of(n, k, x)
        mix[head, rows_of(tok), :] = attend(m, tok)
        mg.first(n)

        @pl.when(n >= 3)
        def _():
            mg.second(n - 3, (n - 3) % 2 == 0)
        return carry

    lax.fori_loop(0, 6, step_one, 0)

    def widen(t):
        rows = rows_of(t * QB)
        gated(hid, rows, t * QB, [mix[h, rows, :] for h in range(HEADS)], ends, gate_w)
        project(t)

    for n in range(3):
        hg.drain(n)
    mg.second(3, False)
    mg.second(4, True)
    mg.third(0)
    mg.third(1)
    mg.second(5, False)
    mg.last(0)
    mg.last(1)
    widen(0)
    mg.third(2)
    mg.third(3)
    mg.last(2)
    widen(2)
    mg.third(4)
    mg.third(5)
    mg.last(3)
    mg.last(4)
    widen(1)
    mg.last(5)
    widen(3)

    home_local = pltpu.make_async_copy(hid.at[rows_of(p * TOK, TOK), :], home, home_recv)
    home_copy = remote(hid.at[rows_of(p4 * TOK, TOK), :], home, home_send, home_recv, partner)

    @pl.when(same)
    def _():
        home_local.start()

    @pl.when(apart)
    def _():
        home_copy.start()

    def piece(n, half, sent):
        m, head, tok = item_of(n, k, x)
        d = tok // TOK + half
        src = mine.at[n, pl.ds(half * TOK, TOK), :]
        here = jnp.logical_and(same, d == p)

        if not sent:
            @pl.when(here)
            def _():
                pltpu.make_async_copy(src, fin.at[head], aa_recv.at[head]).start()

        @pl.when(jnp.logical_not(here))
        def _():
            copy = remote(src, fin.at[head], aa_send.at[n, half], aa_recv.at[head], (work_g, d))
            if sent:
                copy.wait_send()
            else:
                copy.start()

    def step_two(n, carry):
        m, head, tok = item_of(n, k, x)
        mine[n] = attend(m, tok)
        for half in (0, 1):
            piece(n, half, False)
        return carry

    lax.fori_loop(0, 6, step_two, 0)

    def take_head(h, carry):
        remote(fin.at[h], fin.at[h], aa_send.at[0, 0], aa_recv.at[h], core).wait_recv()
        return carry

    lax.fori_loop(0, HEADS, take_head, 0)
    home_copy.wait_recv()
    gated(home, pl.ds(0, TOK), p * TOK, [fin[h] for h in range(HEADS)], own_ends, gate)
    back[z, :, 0:WIDTH] = home[KEEP:TOK, :]
    back[z, :, WIDTH:] = jnp.full((PAGE, TAG), inc[0, 0], jnp.int32).astype(F32).astype(BF16)
    z_first(3, back_at)
    out[0:KEEP, :] = home[0:KEEP, :]
    for step in (1, 2, 3, 4):
        z_step(3, back_at, step, True)

    def want_back(zz, cc):
        return back[zz, :, WIDTH:WIDTH + 1].astype(F32) == (z * 4 + cc).astype(F32)

    route_send(back, 1, want_back)
    out[KEEP:TOK, :] = route_take(1)

    for copy in pending:
        copy.wait_send()
    route_drain(0)
    route_drain(1)

    @pl.when(same)
    def _():
        shared_copies(lambda copy: copy.wait_send())

    @pl.when(apart)
    def _():
        home_copy.wait_send()
        for n in range(2):
            part_copy(n).wait_send()

    def drain(n, carry):
        mg.drain(n)
        for half in (0, 1):
            piece(n, half, True)
        return carry

    lax.fori_loop(0, 6, drain, 0)


def shards(latent, incoming, req_pages, text_len, gate_scale, text_keys, text_values, w_query, w_key, w_value, w_out):
    vm = pl.BlockSpec(memory_space=pltpu.VMEM)
    hb = pl.BlockSpec(memory_space=pltpu.HBM)
    dma = pltpu.SemaphoreType.DMA
    return pl.pallas_call(
        kernel,
        out_shape=jax.ShapeDtypeStruct((TOK, WIDTH), BF16),
        in_specs=[hb] * 11,
        out_specs=vm,
        scratch_shapes=[
            pltpu.VMEM((SEQ, WIDTH), BF16),
            pltpu.VMEM((TOK, WIDTH), BF16),
            pltpu.VMEM((3, WIDTH, 3 * DIM), BF16),
            pltpu.VMEM((WIDTH, WIDTH), BF16),
            pltpu.VMEM((HEADS, SEQ, DIM), BF16),
            pltpu.VMEM((2, KEYS, DIM), BF16),
            pltpu.VMEM((2, KEYS, DIM), BF16),
            pltpu.VMEM((2, SEQ, DIM), BF16),
            pltpu.VMEM((6, QB, DIM), BF16),
            pltpu.VMEM((HEADS, TOK, DIM), BF16),
            pltpu.VMEM((8, KEYS), jnp.int32),
            pltpu.VMEM((NZ, PAGE, WIDTH), BF16),
            pltpu.VMEM((NZ, PAGE, WIDTH + TAG), BF16),
            pltpu.VMEM((32, 8, 128), jnp.int32),
            pltpu.VMEM((2, 4, PAGE, WIDTH), BF16),
            pltpu.VMEM((2, 4, PAGE, WIDTH), BF16),
            pltpu.VMEM((2 * REQS, 8, 128), jnp.int32),
            pltpu.VMEM((REQS, WIDTH), F32),
            pltpu.SMEM((1, 1), jnp.int32),
            pltpu.SMEM((1, REQS), jnp.int32),
            pltpu.SMEM((1, REQS), jnp.int32),
            pltpu.VMEM((REQS, WIDTH), F32),
            dma((21,)),
            dma((4, 7)), dma((4, 7)),
            dma((2, NZ)), dma((2, NZ)),
            dma, dma,
            dma((3,)), dma((3,)),
            dma((2, 4)), dma((2, 4)),
            dma((2,)), dma((2,)),
            dma((6,)), dma((6,)),
            dma((3, 7)), dma((3, 7)),
            dma((6, 7)), dma((6, 7)),
            dma, dma,
            dma((6, 2)), dma((HEADS,)),
        ],
        compiler_params=pltpu.CompilerParams(
            collective_id=0, has_side_effects=True, vmem_limit_bytes=56 * 1024 * 1024),
        cost_estimate=pl.CostEstimate(flops=14_000_000_000, bytes_accessed=10_000_000, transcendentals=5_000_000),
    )(
        latent, incoming, req_pages, text_len, gate_scale[0],
        text_keys.reshape(REQS * TXT, WIDTH), text_values.reshape(REQS * TXT, WIDTH),
        w_query, w_key, w_value, w_out,
    )


def solution(mesh):
    in_specs = (
        P(("grp", "patch"), None),
        P("patch", "grp"),
        P("grp", None),
        P("grp", None),
        P("grp", None, None),
        P("grp", None, None, None),
        P("grp", None, None, None),
        P("grp", None),
        P("grp", None),
        P("grp", None),
        P(),
    )
    return jax.shard_map(
        shards, mesh=mesh, in_specs=in_specs, out_specs=P(("grp", "patch"), None), check_vma=False)
```

time: 129 us -> 102 us (0.79)
  Pallas kernels: 119 us -> 99.1 us
  local copies, waits for them, and re-layouts: 7.92 us -> 1.77 us
    pallas_call x1, Pallas kernels: 119 us -> 99.1 us  [shards(): pl.pallas_call(kernel, out_shape=jax.ShapeDtypeStruct((TOK, WIDTH), BF16)...]
    unnamed x17 -> x1, local copies, waits for them, and re-layouts: 7.92 us -> 1.77 us
where the time goes in v2:
time: 102 us
  Pallas kernels  99.1 us (97%)
  local copies, waits for them, and re-layouts  1.77 us (2%)
    pallas_call x1, Pallas kernels, shards(): pl.pallas_call(kernel, out_shape=jax.ShapeDtypeStruct((TOK, WIDTH), BF16)...  99.1 us

profile of v2, /device:TPU:1, one launch (start us, length us, event | category | flops | bytes accessed | tf_op | source)
XLA Modules:
  0.0 101.5 jit_solution(18107967979251543658)
XLA Ops:
  0.7 99.1 %shard_map.109 = bf16[128,1536]{1,0:T(8,128)(2,1)} custom-call(bf16[128,1536]{1,0:T(8,128)(2,1)} %lat.1, s32[1,1]{1,0:T(1,128)S(6)} %copy.13.inc_h, s32[1,4]{1,0:T(1,128)} %req_pages_h.1, s32[1,4]{1,0:T(1,128)} %text_len_h.1, f32[4,1536]{1,0:T(4,128)} %bitcast.5, bf16[512,1536]{1,0:T(8,128)(2,1)} %bitcast.3, bf16[512,1536]{1,0:T(8,128)(2,1)} %bitcast.4, ...), custom_call_target="tpu_custom_call" | custom-call | flops 14000000000 | bytes 10000000 | tf_op jit(solution)/shard_map/pallas_call | solution.py:595
  99.7 1.8 %copy.14 = bf16[128,1536]{1,0:T(8,128)(2,1)} copy(bf16[128,1536]{1,0:T(8,128)(2,1)} %shard_map.109) | data formatting | bytes 786432

commit v3 on v2

--- a/solution.py
+++ b/solution.py
@@ -19,6 +19,7 @@
 KEEP = TOK - PAGE
 NZ = 8
 WROWS = 48
+BLOCKS = 10
 KEYS = SEQ + REQS * TXT
 QB = 256
 NEG_FILL = -1e30
@@ -32,11 +33,11 @@
 
 def kernel(
     lat, inc_h, req_pages_h, text_len_h, gate_h, text_k, text_v, w_q, w_k, w_v, w_o, out,
-    hid, home, wgt, wout, mix, keys, vals, qry, mine, fin, kid,
+    hid, home, wgt, wout, mix, keys, vals, qry, mine, fin, mine_page, fin_page, kid,
     pages, back, ints, pick_out, pick_in, info, gate_w,
-    inc, req_pages, text_len, gate, local_sem, z_send, z_recv, swap_send, swap_recv, yh_send, yh_recv,
+    inc, req_pages, text_len, gate, local_sem, weight_sem, z_send, z_recv, swap_send, swap_recv, cross_send, cross_recv, pair_send, pair_recv,
     int_send, int_recv, set_send, set_recv, part_send, part_recv, text_send, text_recv,
-    hg_send, hg_recv, mg_send, mg_recv, home_send, home_recv, aa_send, aa_recv,
+    hg_send, hg_recv, mg_send, mg_recv, home_send, home_recv, aa_send, aa_recv, pa_send, pa_recv,
 ):
     g = lax.axis_index("grp")
     p = lax.axis_index("patch")
@@ -51,8 +52,11 @@
 
     right, left, far = (g, yl * 4 + (x + 1) % 4), (g, yl * 4 + (x + 3) % 4), (g, yl * 4 + (x + 2) % 4)
     up, down = ((g + 4) % 32, p), ((g + 28) % 32, p)
+    up2, down2 = ((g + 8) % 32, p), ((g + 24) % 32, p)
     yhi_g = z * 4 + (c + 2) % 4
-    core, yhi, partner = (core_g, p), (yhi_g, p), (core_g, p4)
+    core, partner = (core_g, p), (core_g, p4)
+    pair, cross = (g, p4), (yhi_g, p4)
+    mine_first, other_first = 5 * yl, 5 - 5 * yl
 
     def set_peer(j):
         return z * 4 + (c + j) % 4
@@ -65,15 +69,14 @@
     def cols_of(head):
         return pl.ds(pl.multiple_of(head * DIM, DIM), DIM)
 
-    def wrows(gg, first=0, count=3):
+    def wrows(gg, first=0, count=BLOCKS):
         return wgt.at[pl.ds(first, count), pl.ds(pl.multiple_of(gg * WROWS, 16), WROWS), :]
 
+    my_rows = pl.ds(pl.multiple_of(g * WROWS, 16), WROWS)
     loads = []
-    my_rows = pl.ds(pl.multiple_of(g * WROWS, 16), WROWS)
-    for n, w in enumerate((w_q, w_k, w_v)):
-        for h in range(3):
-            loads.append(pltpu.make_async_copy(
-                w.at[:, cols_of(3 * x + h)], wgt.at[h, my_rows, pl.ds(n * DIM, DIM)], local_sem.at[3 * n + h]))
+    for b in range(BLOCKS):
+        w = (w_q, w_k, w_v)[b % 3]
+        loads.append(pltpu.make_async_copy(w.at[:, cols_of(3 * x + b // 3 % 3)], wgt.at[b, my_rows, :], weight_sem.at[b]))
     my_hid = pl.ds(pl.multiple_of(p * TOK, TOK), KEEP)
 
     def text_copies(fn, heads):
@@ -82,21 +85,21 @@
                 fn(src.at[:, cols_of(heads[m])], dst.at[m, pl.ds(SEQ, REQS * TXT), :], 2 * n + m)
 
     def own_loads(fn):
-        text_copies(lambda src, dst, n: fn(pltpu.make_async_copy(src, dst, local_sem.at[9 + n])), (head_a, head_b))
-        fn(pltpu.make_async_copy(lat.at[pl.ds(0, KEEP), :], hid.at[my_hid, :], local_sem.at[13]))
-        fn(pltpu.make_async_copy(gate_h, gate_w, local_sem.at[14]))
-
-    wout_load = pltpu.make_async_copy(w_o, wout, local_sem.at[15])
-    page_load = pltpu.make_async_copy(lat.at[pl.ds(KEEP, PAGE), :], pages.at[z], local_sem.at[16])
+        text_copies(lambda src, dst, n: fn(pltpu.make_async_copy(src, dst, local_sem.at[n])), (head_a, head_b))
+        fn(pltpu.make_async_copy(lat.at[pl.ds(0, KEEP), :], hid.at[my_hid, :], local_sem.at[4]))
+        fn(pltpu.make_async_copy(gate_h, gate_w, local_sem.at[5]))
+
+    wout_load = pltpu.make_async_copy(w_o, wout, local_sem.at[6])
+    page_load = pltpu.make_async_copy(lat.at[pl.ds(KEEP, PAGE), :], pages.at[z], local_sem.at[7])
     small_loads = [
-        pltpu.make_async_copy(src, dst, local_sem.at[17 + n])
+        pltpu.make_async_copy(src, dst, local_sem.at[8 + n])
         for n, (src, dst) in enumerate(((inc_h, inc), (req_pages_h, req_pages), (text_len_h, text_len), (gate_h, gate)))]
     page_load.start()
     for load in small_loads + loads:
         load.start()
 
     barrier = pltpu.get_barrier_semaphore()
-    greeted = [up, down]
+    greeted = [up, down, up2, down2]
     plane = z * 4 + yh * 2
     for dk in range(2):
         for dp in range(8):
@@ -158,18 +161,30 @@
         return back.at[(z + dz) % NZ]
 
     def own_w(dz):
-        return wrows(zdev(dz, c))
+        return wrows(zdev(dz, c), mine_first, 5)
 
     def yhi_w(dz):
-        return wrows(zdev(dz, (c + 2) % 4))
+        return wrows(zdev(dz, (c + 2) % 4), mine_first, 5)
+
+    def y_go(dz):
+        go(own_w(dz), own_w(dz), pair_send.at[dz % NZ], pair_recv.at[dz % NZ], pair)
+        go(own_w(dz), own_w(dz), cross_send.at[dz % NZ], cross_recv.at[dz % NZ], cross)
+
+    def y_take(dz):
+        ref = wrows(zdev(dz, c), other_first, 5)
+        remote(ref, ref, pair_send.at[dz % NZ], pair_recv.at[dz % NZ], pair).wait_recv()
+        cross_take(dz)
+
+    def cross_take(dz):
+        ref = wrows(zdev(dz, (c + 2) % 4), other_first, 5)
+        remote(ref, ref, cross_send.at[dz % NZ], cross_recv.at[dz % NZ], cross).wait_recv()
 
     def swap(item, dz):
-        ref = wrows(zdev(dz, (c + 2 * item) % 4), 1 - k, 2)
+        ref = wrows(zdev(dz, (c + 2 * item) % 4))
         go(ref, ref, swap_send.at[item, dz % NZ], swap_recv.at[item, dz % NZ], core)
 
     def swap_wait(item, dz):
-        other_c = 2 * yh + 1 - k
-        ref = wrows(zdev(dz, (other_c + 2 * item) % 4), k, 2)
+        ref = wrows(zdev(dz, (2 * yh + 1 - k + 2 * item) % 4))
         remote(ref, ref, swap_send.at[item, dz % NZ], swap_recv.at[item, dz % NZ], core).wait_recv()
 
     X_FROM = (3, 1, 2, 0, 3, 1, 2)
@@ -260,7 +275,9 @@
     for load in loads:
         load.wait()
     z_first(1, own_w)
-    go(wrows(g), wrows(g), yh_send, yh_recv, yhi)
+    other_half = wrows(g, other_first, 5)
+    go(other_half, other_half, cross_send.at[NZ], cross_recv.at[NZ], cross)
+    go(own_w(0), own_w(0), cross_send.at[0], cross_recv.at[0], cross)
     for load in small_loads:
         load.wait()
     ints[g] = jnp.full((8, 128), inc[0, 0], jnp.int32)
@@ -300,12 +317,15 @@
         return remote(pick_out.at[kind, cc], pick_in.at[kind, slot], set_send.at[kind, cc], set_recv.at[kind, slot], dev)
 
     def route_send(ring, kind, want):
+        for col in range(0, WIDTH, 512):
+            accs = [jnp.zeros((PAGE, 512), F32)] * 4
+            for zz in range(NZ):
+                page = ring[zz, :, col:col + 512].astype(F32)
+                accs = [jnp.where(want(zz, cc), page, accs[cc]) for cc in range(4)]
+            for cc in range(4):
+                pick_out[kind, cc, :, col:col + 512] = accs[cc].astype(BF16)
         for cc in range(4):
-            acc = jnp.zeros((PAGE, WIDTH), F32)
-            for zz in range(NZ):
-                acc = acc + jnp.where(want(zz, cc), ring[zz, :, 0:WIDTH].astype(F32), 0.0)
             dev, here = route_to(kind, cc)
-            pick_out[kind, cc] = acc.astype(BF16)
 
             @pl.when(jnp.logical_not(here))
             def _():
@@ -313,7 +333,7 @@
 
             @pl.when(here)
             def _():
-                pick_in[kind, cc] = acc.astype(BF16)
+                pick_in[kind, cc] = pick_out[kind, cc]
 
     def route_take(kind):
         for cc in range(4):
@@ -334,10 +354,11 @@
         return ints[z * 4 + cc, 0:1, 0:1] == zz * 4 + c
 
     z_step(0, page_at, 1, True)
+    remote(yhi_w(0), yhi_w(0), cross_send.at[NZ], cross_recv.at[NZ], cross).wait_recv()
+    z_first(2, yhi_w)
     z_step(1, own_w, 1, True)
-    remote(wrows(yhi_g), wrows(yhi_g), yh_send, yh_recv, yhi).wait_recv()
-    z_first(2, yhi_w)
-    swap(1, 0)
+    y_go(-1)
+    y_go(1)
 
     @pl.when(apart)
     def _():
@@ -346,36 +367,42 @@
             hg.first(n)
 
     z_step(0, page_at, 2, True)
-    for dz in (-1, 1):
-        swap(0, dz)
+    z_step(2, yhi_w, 1, False)
     z_step(1, own_w, 2, True)
-    z_step(2, yhi_w, 1, False)
+    y_go(-2)
+    y_go(2)
+    cross_take(0)
+    swap(1, 0)
     z_step(0, page_at, 3, True)
-    for dz in (-2, 2):
-        swap(0, dz)
-    for dz in (-1, 1):
-        swap(1, dz)
+    z_step(2, yhi_w, 2, False)
+    z_step(1, own_w, 3, True)
+    y_go(-3)
+    y_go(3)
     hg.second(0, True)
     hg.second(1, False)
-    z_step(1, own_w, 3, True)
-    z_step(2, yhi_w, 2, False)
     z_step(0, page_at, 4, True)
     for j in (1, 2, 3):
         src = set_peer(4 - j)
         remote(ints.at[src], ints.at[src], int_send.at[j - 1], int_recv.at[j - 1], core).wait_recv()
     route_send(pages, 0, want_in)
     z_step(2, yhi_w, 3, False)
-    for dz in (-3, 3):
+    z_step(1, own_w, 4, True)
+    y_go(4)
+    for dz in (-1, 1, -2, 2):
+        y_take(dz)
         swap(0, dz)
-    for dz in (-2, 2, -3, 3):
         swap(1, dz)
+    hg.third(0)
+    hg.third(1)
     hid[pl.ds(pl.multiple_of((k * 4 + x) * TOK + KEEP, 16), PAGE), :] = route_take(0)
     hg.direct(2)
-    hg.third(0)
-    hg.third(1)
-    z_step(1, own_w, 4, True)
+    for dz in (-3, 3):
+        y_take(dz)
+        swap(0, dz)
+        swap(1, dz)
+    z_step(2, yhi_w, 4, False)
+    y_take(4)
     swap(0, 4)
-    z_step(2, yhi_w, 4, False)
     swap(1, 4)
 
     @pl.when(same)
@@ -413,18 +440,16 @@
 
     def project(t):
         rows = rows_of(t * QB)
-        w = jnp.concatenate([wgt[2 * k], wgt[1]], axis=1)
+        w = jnp.concatenate([wgt[6 * k + n] for n in range(3)] + [wgt[3 + n] for n in range(3)], axis=1)
         y = jnp.dot(hid[rows, :], w, preferred_element_type=F32).astype(BF16)
         for m in range(2):
             qry[m, rows, :] = y[:, (3 * m) * DIM:(3 * m + 1) * DIM]
             keys[m, rows, :] = y[:, (3 * m + 1) * DIM:(3 * m + 2) * DIM]
             vals[m, rows, :] = y[:, (3 * m + 2) * DIM:(3 * m + 3) * DIM]
 
-    def attend(m, tok):
-        q = qry[m, rows_of(tok), :]
+    def attend(q, pos, m):
         s = lax.dot_general(q, keys[m], (((1,), (1,)), ((), ())), preferred_element_type=F32)
-        qseg = segment(tok + lax.broadcasted_iota(jnp.int32, (QB, 1), 0), ends)
-        s = jnp.where(qseg == kid[0:1, :], s, NEG_FILL)
+        s = jnp.where(segment(pos, ends) == kid[0:1, :], s, NEG_FILL)
         best = jnp.max(s, axis=1, keepdims=True)
         w = jnp.exp2((s - best) * EXP_SCALE)
         total_w = jnp.sum(w, axis=1, keepdims=True)
@@ -468,7 +493,8 @@
 
     def step_one(n, carry):
         m, head, tok = item_of(n, k, x)
-        mix[head, rows_of(tok), :] = attend(m, tok)
+        pos = tok + lax.broadcasted_iota(jnp.int32, (QB, 1), 0)
+        mix[head, rows_of(tok), :] = attend(qry[m, rows_of(tok), :], pos, m)
         mg.first(n)
 
         @pl.when(n >= 3)
@@ -516,47 +542,109 @@
     def _():
         home_copy.start()
 
-    def piece(n, half, sent):
-        m, head, tok = item_of(n, k, x)
-        d = tok // TOK + half
-        src = mine.at[n, pl.ds(half * TOK, TOK), :]
+    def send_home(src, dst, send, recv, d, sent):
         here = jnp.logical_and(same, d == p)
 
         if not sent:
             @pl.when(here)
             def _():
-                pltpu.make_async_copy(src, fin.at[head], aa_recv.at[head]).start()
+                pltpu.make_async_copy(src, dst, recv).start()
 
         @pl.when(jnp.logical_not(here))
         def _():
-            copy = remote(src, fin.at[head], aa_send.at[n, half], aa_recv.at[head], (work_g, d))
+            copy = remote(src, dst, send, recv, (work_g, d))
             if sent:
                 copy.wait_send()
             else:
                 copy.start()
 
+    def page_piece(n, sent):
+        head = 3 * x + jnp.where(n < 8, 2 * k, 1)
+        d = jnp.where(n < 8, n, k * 4 + n - 8)
+        send_home(mine_page.at[n], fin_page.at[head], pa_send.at[n], pa_recv.at[head], d, sent)
+
+    def piece(n, half, sent):
+        m = (n >= 4).astype(jnp.int32)
+        head = 3 * x + jnp.where(n < 4, 2 * k, 1)
+        d = jnp.where(n < 4, 2 * n, k * 4 + 2 * (n - 4)) + half
+        send_home(mine.at[n, half], fin.at[head], aa_send.at[n, half], aa_recv.at[head], d, sent)
+        return m, d
+
+    def block_pos(rows, block, first):
+        i = lax.broadcasted_iota(jnp.int32, (rows, 1), 0)
+        return first + i + (i // block) * (TOK - block)
+
+    for m, count, first in ((0, 8, 0), (1, 4, k * 4)):
+        q = jnp.concatenate(
+            [qry[m, pl.ds(pl.multiple_of((first + j) * TOK + KEEP, 16), PAGE), :] for j in range(count)], axis=0)
+        o = attend(q, block_pos(count * PAGE, PAGE, first * TOK + KEEP), m)
+        for j in range(count):
+            mine_page[8 * m + j] = o[j * PAGE:(j + 1) * PAGE]
+
+    def send_page(n, carry):
+        page_piece(n, False)
+        return carry
+
+    lax.fori_loop(0, 12, send_page, 0)
+
     def step_two(n, carry):
-        m, head, tok = item_of(n, k, x)
-        mine[n] = attend(m, tok)
+        m = (n >= 4).astype(jnp.int32)
+        d = jnp.where(n < 4, 2 * n, k * 4 + 2 * (n - 4))
+        q = jnp.concatenate(
+            [qry[m, pl.ds(pl.multiple_of((d + j) * TOK, 128), KEEP), :] for j in range(2)], axis=0)
+        o = attend(q, block_pos(2 * KEEP, KEEP, d * TOK), m)
+        for half in (0, 1):
+            mine[n, half] = o[half * KEEP:(half + 1) * KEEP]
         for half in (0, 1):
             piece(n, half, False)
         return carry
 
-    lax.fori_loop(0, 6, step_two, 0)
-
-    def take_head(h, carry):
-        remote(fin.at[h], fin.at[h], aa_send.at[0, 0], aa_recv.at[h], core).wait_recv()
-        return carry
-
-    lax.fori_loop(0, HEADS, take_head, 0)
+    def take_heads(ref, recv):
+        def take(h, carry):
+            remote(ref.at[h], ref.at[h], aa_send.at[0, 0], recv.at[h], core).wait_recv()
+            return carry
+
+        lax.fori_loop(0, HEADS, take, 0)
+
+    lax.fori_loop(0, 2, step_two, 0)
+    take_heads(fin_page, pa_recv)
     home_copy.wait_recv()
-    gated(home, pl.ds(0, TOK), p * TOK, [fin[h] for h in range(HEADS)], own_ends, gate)
+    gated(home, pl.ds(KEEP, PAGE), p * TOK + KEEP, [fin_page[h] for h in range(HEADS)], own_ends, gate)
     back[z, :, 0:WIDTH] = home[KEEP:TOK, :]
     back[z, :, WIDTH:] = jnp.full((PAGE, TAG), inc[0, 0], jnp.int32).astype(F32).astype(BF16)
+
+    def half_at(dz, first, count):
+        return back.at[(z + dz) % NZ, :, pl.ds(first, count)]
+
+    HALVES = ((6, 0, WIDTH // 2), (7, WIDTH // 2, WIDTH // 2 + TAG))
+
+    def half_copy(n, dz, dev):
+        slot, first, count = HALVES[n]
+        ref = half_at(dz, first, count)
+        return remote(ref, ref, z_send.at[3, slot], z_recv.at[3, slot], dev)
+
+    def half_go(n, dz, dev):
+        copy = half_copy(n, dz, dev)
+        copy.start()
+        pending.append(copy)
+
+    z_go(3, back_at, 1, 0, up2)
+    z_go(3, back_at, 4, 0, down2)
     z_first(3, back_at)
+    lax.fori_loop(2, 6, step_two, 0)
+    z_wait(3, back_at, 1)
+    half_go(0, -2, up2)
+    z_go(3, back_at, 2, -2, up)
+    z_wait(3, back_at, 4)
+    half_go(1, 2, down2)
+    z_go(3, back_at, 5, 2, down)
+    take_heads(fin, aa_recv)
+    gated(home, pl.ds(0, KEEP), p * TOK, [fin[h] for h in range(HEADS)], own_ends, gate)
     out[0:KEEP, :] = home[0:KEEP, :]
-    for step in (1, 2, 3, 4):
-        z_step(3, back_at, step, True)
+    for slot in (0, 3, 2, 5):
+        z_wait(3, back_at, slot)
+    for n in (0, 1):
+        half_copy(n, 4, up).wait_recv()
 
     def want_back(zz, cc):
         return back[zz, :, WIDTH:WIDTH + 1].astype(F32) == (z * 4 + cc).astype(F32)
@@ -583,6 +671,7 @@
         mg.drain(n)
         for half in (0, 1):
             piece(n, half, True)
+            page_piece(2 * n + half, True)
         return carry
 
     lax.fori_loop(0, 6, drain, 0)
@@ -600,14 +689,16 @@
         scratch_shapes=[
             pltpu.VMEM((SEQ, WIDTH), BF16),
             pltpu.VMEM((TOK, WIDTH), BF16),
-            pltpu.VMEM((3, WIDTH, 3 * DIM), BF16),
+            pltpu.VMEM((BLOCKS, WIDTH, DIM), BF16),
             pltpu.VMEM((WIDTH, WIDTH), BF16),
             pltpu.VMEM((HEADS, SEQ, DIM), BF16),
             pltpu.VMEM((2, KEYS, DIM), BF16),
             pltpu.VMEM((2, KEYS, DIM), BF16),
             pltpu.VMEM((2, SEQ, DIM), BF16),
-            pltpu.VMEM((6, QB, DIM), BF16),
-            pltpu.VMEM((HEADS, TOK, DIM), BF16),
+            pltpu.VMEM((6, 2, KEEP, DIM), BF16),
+            pltpu.VMEM((HEADS, KEEP, DIM), BF16),
+            pltpu.VMEM((12, PAGE, DIM), BF16),
+            pltpu.VMEM((HEADS, PAGE, DIM), BF16),
             pltpu.VMEM((8, KEYS), jnp.int32),
             pltpu.VMEM((NZ, PAGE, WIDTH), BF16),
             pltpu.VMEM((NZ, PAGE, WIDTH + TAG), BF16),
@@ -620,10 +711,11 @@
             pltpu.SMEM((1, REQS), jnp.int32),
             pltpu.SMEM((1, REQS), jnp.int32),
             pltpu.VMEM((REQS, WIDTH), F32),
-            dma((21,)),
-            dma((4, 7)), dma((4, 7)),
+            dma((12,)), dma((BLOCKS,)),
+            dma((4, 8)), dma((4, 8)),
             dma((2, NZ)), dma((2, NZ)),
-            dma, dma,
+            dma((NZ + 1,)), dma((NZ + 1,)),
+            dma((NZ,)), dma((NZ,)),
             dma((3,)), dma((3,)),
             dma((2, 4)), dma((2, 4)),
             dma((2,)), dma((2,)),
@@ -632,6 +724,7 @@
             dma((6, 7)), dma((6, 7)),
             dma, dma,
             dma((6, 2)), dma((HEADS,)),
+            dma((12,)), dma((HEADS,)),
         ],
         compiler_params=pltpu.CompilerParams(
             collective_id=0, has_side_effects=True, vmem_limit_bytes=56 * 1024 * 1024),

time: 102 us -> 93.6 us (0.918)
  Pallas kernels: 99.1 us -> 91 us
    pallas_call x1, Pallas kernels: 99.1 us -> 91 us  [shards(): pl.pallas_call(kernel, out_shape=jax.ShapeDtypeStruct((TOK, WIDTH), BF16)...]
where the time goes in v3:
time: 93.6 us; the launch traced here: 93.4 us
  Pallas kernels  91 us (97%)
  local copies, waits for them, and re-layouts  1.77 us (2%)
    pallas_call x1, Pallas kernels, shards(): pl.pallas_call(kernel, out_shape=jax.ShapeDtypeStruct((TOK, WIDTH), BF16)...  91 us

profile of v3, /device:TPU:1, one launch (start us, length us, event | category | flops | bytes accessed | tf_op | source)
XLA Modules:
  0.0 93.4 jit_solution(18004552387647195675)
XLA Ops:
  0.7 91.0 %shard_map.109 = bf16[128,1536]{1,0:T(8,128)(2,1)} custom-call(bf16[128,1536]{1,0:T(8,128)(2,1)} %lat.1, s32[1,1]{1,0:T(1,128)S(6)} %copy.13.inc_h, s32[1,4]{1,0:T(1,128)} %req_pages_h.1, s32[1,4]{1,0:T(1,128)} %text_len_h.1, f32[4,1536]{1,0:T(4,128)} %bitcast.5, bf16[512,1536]{1,0:T(8,128)(2,1)} %bitcast.3, bf16[512,1536]{1,0:T(8,128)(2,1)} %bitcast.4, ...), custom_call_target="tpu_custom_call" | custom-call | flops 14000000000 | bytes 10000000 | tf_op jit(solution)/shard_map/pallas_call | solution.py:684
  91.7 1.8 %copy.14 = bf16[128,1536]{1,0:T(8,128)(2,1)} copy(bf16[128,1536]{1,0:T(8,128)(2,1)} %shard_map.109) | data formatting | bytes 786432

commit v4 on v3

--- a/solution.py
+++ b/solution.py
@@ -154,11 +154,37 @@
         elif not last_up:
             z_go(item, at, 6, 3, down)
 
-    def page_at(dz):
-        return pages.at[(z + dz) % NZ]
-
-    def back_at(dz):
-        return back.at[(z + dz) % NZ]
+    def two_copy(item, slot, dz, dev, src=None):
+        ring, first, count = pages if item == 0 else back, 0, WIDTH + (TAG if item else 0)
+        if slot == 6:
+            count = WIDTH // 2
+        if slot == 7:
+            first, count = WIDTH // 2, count - WIDTH // 2
+        ref = ring.at[(z + dz) % NZ, :, pl.ds(first, count)]
+        return remote(ref if src is None else src, ref, z_send.at[item, slot], z_recv.at[item, slot], dev)
+
+    def two_go(item, slot, dz, dev, src=None):
+        copy = two_copy(item, slot, dz, dev, src)
+        copy.start()
+        pending.append(copy)
+
+    def two_first(item, src=None):
+        two_go(item, 1, 0, up2, src)
+        two_go(item, 4, 0, down2, src)
+        two_go(item, 0, 0, up, src)
+        two_go(item, 3, 0, down, src)
+
+    def two_second(item):
+        two_copy(item, 1, -2, up).wait_recv()
+        two_go(item, 6, -2, up2)
+        two_go(item, 2, -2, up)
+        two_copy(item, 4, 2, up).wait_recv()
+        two_go(item, 7, 2, down2)
+        two_go(item, 5, 2, down)
+
+    def two_last(item):
+        for slot, dz in ((0, -1), (3, 1), (2, -3), (5, 3), (6, 4), (7, 4)):
+            two_copy(item, slot, dz, up).wait_recv()
 
     def own_w(dz):
         return wrows(zdev(dz, c), mine_first, 5)
@@ -259,8 +285,7 @@
     def part_taken(n):
         return remote(lat_part(n), hid_at(n, k, x), part_send.at[n], part_recv.at[n], partner)
 
-    page_load.wait()
-    z_first(0, page_at)
+    two_first(0, lat.at[pl.ds(KEEP, PAGE), :])
 
     @pl.when(same)
     def _():
@@ -353,12 +378,12 @@
     def want_in(zz, cc):
         return ints[z * 4 + cc, 0:1, 0:1] == zz * 4 + c
 
-    z_step(0, page_at, 1, True)
     remote(yhi_w(0), yhi_w(0), cross_send.at[NZ], cross_recv.at[NZ], cross).wait_recv()
     z_first(2, yhi_w)
     z_step(1, own_w, 1, True)
     y_go(-1)
     y_go(1)
+    two_second(0)
 
     @pl.when(apart)
     def _():
@@ -366,36 +391,35 @@
             part_taken(n).wait_recv()
             hg.first(n)
 
-    z_step(0, page_at, 2, True)
     z_step(2, yhi_w, 1, False)
     z_step(1, own_w, 2, True)
     y_go(-2)
     y_go(2)
     cross_take(0)
     swap(1, 0)
-    z_step(0, page_at, 3, True)
+    for j in (1, 2, 3):
+        src = set_peer(4 - j)
+        remote(ints.at[src], ints.at[src], int_send.at[j - 1], int_recv.at[j - 1], core).wait_recv()
+    page_load.wait()
+    two_last(0)
+    route_send(pages, 0, want_in)
     z_step(2, yhi_w, 2, False)
     z_step(1, own_w, 3, True)
     y_go(-3)
     y_go(3)
     hg.second(0, True)
     hg.second(1, False)
-    z_step(0, page_at, 4, True)
-    for j in (1, 2, 3):
-        src = set_peer(4 - j)
-        remote(ints.at[src], ints.at[src], int_send.at[j - 1], int_recv.at[j - 1], core).wait_recv()
-    route_send(pages, 0, want_in)
     z_step(2, yhi_w, 3, False)
     z_step(1, own_w, 4, True)
     y_go(4)
+    hid[pl.ds(pl.multiple_of((k * 4 + x) * TOK + KEEP, 16), PAGE), :] = route_take(0)
+    hg.direct(2)
     for dz in (-1, 1, -2, 2):
         y_take(dz)
         swap(0, dz)
         swap(1, dz)
     hg.third(0)
     hg.third(1)
-    hid[pl.ds(pl.multiple_of((k * 4 + x) * TOK + KEEP, 16), PAGE), :] = route_take(0)
-    hg.direct(2)
     for dz in (-3, 3):
         y_take(dz)
         swap(0, dz)
@@ -432,20 +456,23 @@
     for item in (0, 1):
         for dz in range(NZ):
             swap_wait(item, dz)
-    for n in range(3):
+    for n in range(2):
         hg.last(n)
 
     def rows_of(start, size=QB):
         return pl.ds(pl.multiple_of(start, 128), size)
 
-    def project(t):
-        rows = rows_of(t * QB)
+    def project(blocks):
+        at = [pl.ds(pl.multiple_of(first, 16), size) for first, size in blocks]
         w = jnp.concatenate([wgt[6 * k + n] for n in range(3)] + [wgt[3 + n] for n in range(3)], axis=1)
-        y = jnp.dot(hid[rows, :], w, preferred_element_type=F32).astype(BF16)
-        for m in range(2):
-            qry[m, rows, :] = y[:, (3 * m) * DIM:(3 * m + 1) * DIM]
-            keys[m, rows, :] = y[:, (3 * m + 1) * DIM:(3 * m + 2) * DIM]
-            vals[m, rows, :] = y[:, (3 * m + 2) * DIM:(3 * m + 3) * DIM]
+        a = jnp.concatenate([hid[rows, :] for rows in at], axis=0)
+        y = jnp.dot(a, w, preferred_element_type=F32).astype(BF16)
+        done = 0
+        for rows, (_, size) in zip(at, blocks):
+            for n, ref in enumerate((qry, keys, vals)):
+                for m in range(2):
+                    ref[m, rows, :] = y[done:done + size, (3 * m + n) * DIM:(3 * m + n + 1) * DIM]
+            done += size
 
     def attend(q, pos, m):
         s = lax.dot_general(q, keys[m], (((1,), (1,)), ((), ())), preferred_element_type=F32)
@@ -461,16 +488,13 @@
         seg = segment(start + lax.broadcasted_iota(jnp.int32, (size, 1), 0), bounds)
         a = jnp.concatenate(heads, axis=1)
 
-        def tile(n, carry):
-            cols = pl.ds(pl.multiple_of(n * 512, 512), 512)
+        for n in range(3):
+            cols = pl.ds(n * 512, 512)
             proj = jnp.dot(a, wout[:, cols], preferred_element_type=F32)
             scale = gates[3:4, cols]
             for r in (2, 1, 0):
                 scale = jnp.where(seg == r, gates[r:r + 1, cols], scale)
             ref[rows, cols] = (ref[rows, cols].astype(F32) + scale * proj).astype(BF16)
-            return carry
-
-        lax.fori_loop(0, 3, tile, 0)
 
     def item_of(n, kk, xx):
         is_b = jnp.logical_or(n == 1, n == 3)
@@ -485,11 +509,13 @@
 
     mg = Gather(mg_send, mg_recv, mix_at)
 
-    def do_project(t, carry):
-        project(t)
+    def project_kept(t, carry):
+        project([(2 * t * TOK, KEEP), ((2 * t + 1) * TOK, KEEP)])
         return carry
 
-    lax.fori_loop(0, SEQ // QB, do_project, 0)
+    lax.fori_loop(0, 4, project_kept, 0)
+    hg.last(2)
+    project([(d * TOK + KEEP, PAGE) for d in range(8)])
 
     def step_one(n, carry):
         m, head, tok = item_of(n, k, x)
@@ -507,18 +533,18 @@
     def widen(t):
         rows = rows_of(t * QB)
         gated(hid, rows, t * QB, [mix[h, rows, :] for h in range(HEADS)], ends, gate_w)
-        project(t)
+        project([(t * QB, QB)])
 
     for n in range(3):
         hg.drain(n)
+    mg.third(0)
     mg.second(3, False)
-    mg.second(4, True)
-    mg.third(0)
     mg.third(1)
-    mg.second(5, False)
     mg.last(0)
     mg.last(1)
     widen(0)
+    mg.second(4, True)
+    mg.second(5, False)
     mg.third(2)
     mg.third(3)
     mg.last(2)
@@ -613,38 +639,13 @@
     back[z, :, 0:WIDTH] = home[KEEP:TOK, :]
     back[z, :, WIDTH:] = jnp.full((PAGE, TAG), inc[0, 0], jnp.int32).astype(F32).astype(BF16)
 
-    def half_at(dz, first, count):
-        return back.at[(z + dz) % NZ, :, pl.ds(first, count)]
-
-    HALVES = ((6, 0, WIDTH // 2), (7, WIDTH // 2, WIDTH // 2 + TAG))
-
-    def half_copy(n, dz, dev):
-        slot, first, count = HALVES[n]
-        ref = half_at(dz, first, count)
-        return remote(ref, ref, z_send.at[3, slot], z_recv.at[3, slot], dev)
-
-    def half_go(n, dz, dev):
-        copy = half_copy(n, dz, dev)
-        copy.start()
-        pending.append(copy)
-
-    z_go(3, back_at, 1, 0, up2)
-    z_go(3, back_at, 4, 0, down2)
-    z_first(3, back_at)
+    two_first(3)
     lax.fori_loop(2, 6, step_two, 0)
-    z_wait(3, back_at, 1)
-    half_go(0, -2, up2)
-    z_go(3, back_at, 2, -2, up)
-    z_wait(3, back_at, 4)
-    half_go(1, 2, down2)
-    z_go(3, back_at, 5, 2, down)
+    two_second(3)
     take_heads(fin, aa_recv)
     gated(home, pl.ds(0, KEEP), p * TOK, [fin[h] for h in range(HEADS)], own_ends, gate)
     out[0:KEEP, :] = home[0:KEEP, :]
-    for slot in (0, 3, 2, 5):
-        z_wait(3, back_at, slot)
-    for n in (0, 1):
-        half_copy(n, 4, up).wait_recv()
+    two_last(3)
 
     def want_back(zz, cc):
         return back[zz, :, WIDTH:WIDTH + 1].astype(F32) == (z * 4 + cc).astype(F32)
@@ -675,6 +676,10 @@
         return carry
 
     lax.fori_loop(0, 6, drain, 0)
+
+
+def pinned(array):
+    return pltpu.with_memory_space_constraint(array, pltpu.HBM)
 
 
 def shards(latent, incoming, req_pages, text_len, gate_scale, text_keys, text_values, w_query, w_key, w_value, w_out):
@@ -727,12 +732,20 @@
             dma((12,)), dma((HEADS,)),
         ],
         compiler_params=pltpu.CompilerParams(
-            collective_id=0, has_side_effects=True, vmem_limit_bytes=56 * 1024 * 1024),
+            collective_id=0, has_side_effects=True, vmem_limit_bytes=50 * 1024 * 1024),
         cost_estimate=pl.CostEstimate(flops=14_000_000_000, bytes_accessed=10_000_000, transcendentals=5_000_000),
     )(
-        latent, incoming, req_pages, text_len, gate_scale[0],
-        text_keys.reshape(REQS * TXT, WIDTH), text_values.reshape(REQS * TXT, WIDTH),
-        w_query, w_key, w_value, w_out,
+        pinned(latent),
+        incoming,
+        pinned(req_pages),
+        pinned(text_len),
+        pinned(gate_scale[0]),
+        pinned(text_keys.reshape(REQS * TXT, WIDTH)),
+        pinned(text_values.reshape(REQS * TXT, WIDTH)),
+        pinned(w_query),
+        pinned(w_key),
+        pinned(w_value),
+        pinned(w_out),
     )
 
 

time: 93.6 us -> 89 us (0.951)
  Pallas kernels: 91 us -> 87.5 us
  local copies, waits for them, and re-layouts: 1.77 us -> 0.75 us
    pallas_call x1, Pallas kernels: 91 us -> 87.5 us  [shards(): pl.pallas_call(kernel, out_shape=jax.ShapeDtypeStruct((TOK, WIDTH), BF16)...]
    unnamed x1, local copies, waits for them, and re-layouts: 1.77 us -> 0.75 us
where the time goes in v4:
time: 89 us; the launch traced here: 88.9 us
  Pallas kernels  87.5 us (98%)
    pallas_call x1, Pallas kernels, shards(): pl.pallas_call(kernel, out_shape=jax.ShapeDtypeStruct((TOK, WIDTH), BF16)...  87.5 us

profile of v4, /device:TPU:1, one launch (start us, length us, event | category | flops | bytes accessed | tf_op | source)
XLA Modules:
  0.0 88.9 jit_solution(5380106212349914186)
XLA Ops:
  0.7 87.5 %shard_map.109 = bf16[128,1536]{1,0:T(8,128)(2,1)S(1)} custom-call(bf16[128,1536]{1,0:T(8,128)(2,1)} %lat.1, s32[1,1]{1,0:T(1,128)S(6)} %copy.13.inc_h, s32[1,4]{1,0:T(1,128)} %req_pages_h.1, s32[1,4]{1,0:T(1,128)} %text_len_h.1, f32[4,1536]{1,0:T(4,128)} %bitcast.5, bf16[512,1536]{1,0:T(8,128)(2,1)} %bitcast.3, bf16[512,1536]{1,0:T(8,128)(2,1)} %bitcast.4, ...), custom_call_target="tpu_custom_call" | custom-call | flops 14000000000 | bytes 10000000 | tf_op jit(solution)/shard_map/pallas_call | solution.py:689
  88.1 0.7 copy.14

commit v5 on v4

--- a/solution.py
+++ b/solution.py
@@ -285,24 +285,24 @@
     def part_taken(n):
         return remote(lat_part(n), hid_at(n, k, x), part_send.at[n], part_recv.at[n], partner)
 
-    two_first(0, lat.at[pl.ds(KEEP, PAGE), :])
-
-    @pl.when(same)
-    def _():
-        for n in range(2):
-            hg.first(n, lat_part(n))
-
-    @pl.when(apart)
-    def _():
-        for n in range(2):
-            part_copy(n).start()
-
     for load in loads:
         load.wait()
     z_first(1, own_w)
     other_half = wrows(g, other_first, 5)
     go(other_half, other_half, cross_send.at[NZ], cross_recv.at[NZ], cross)
     go(own_w(0), own_w(0), cross_send.at[0], cross_recv.at[0], cross)
+    two_first(0, lat.at[pl.ds(KEEP, PAGE), :])
+
+    @pl.when(same)
+    def _():
+        for n in range(2):
+            hg.first(n, lat_part(n))
+
+    @pl.when(apart)
+    def _():
+        for n in range(2):
+            part_copy(n).start()
+
     for load in small_loads:
         load.wait()
     ints[g] = jnp.full((8, 128), inc[0, 0], jnp.int32)
@@ -523,9 +523,9 @@
         mix[head, rows_of(tok), :] = attend(qry[m, rows_of(tok), :], pos, m)
         mg.first(n)
 
-        @pl.when(n >= 3)
+        @pl.when(n >= 2)
         def _():
-            mg.second(n - 3, (n - 3) % 2 == 0)
+            mg.second(n - 2, (n - 2) % 2 == 0)
         return carry
 
     lax.fori_loop(0, 6, step_one, 0)
@@ -538,12 +538,11 @@
     for n in range(3):
         hg.drain(n)
     mg.third(0)
-    mg.second(3, False)
     mg.third(1)
     mg.last(0)
     mg.last(1)
+    mg.second(4, True)
     widen(0)
-    mg.second(4, True)
     mg.second(5, False)
     mg.third(2)
     mg.third(3)

time: 89 us -> 86.9 us (0.976)
  Pallas kernels: 87.5 us -> 85.5 us
    pallas_call x1, Pallas kernels: 87.5 us -> 85.5 us  [shards(): pl.pallas_call(kernel, out_shape=jax.ShapeDtypeStruct((TOK, WIDTH), BF16)...]
where the time goes in v5:
time: 86.9 us
  Pallas kernels  85.5 us (98%)
    pallas_call x1, Pallas kernels, shards(): pl.pallas_call(kernel, out_shape=jax.ShapeDtypeStruct((TOK, WIDTH), BF16)...  85.5 us

profile of v5, /device:TPU:1, one launch (start us, length us, event | category | flops | bytes accessed | tf_op | source)
XLA Modules:
  0.0 86.9 jit_solution(6706903087545572937)
XLA Ops:
  0.7 85.5 %shard_map.109 = bf16[128,1536]{1,0:T(8,128)(2,1)S(1)} custom-call(bf16[128,1536]{1,0:T(8,128)(2,1)} %lat.1, s32[1,1]{1,0:T(1,128)S(6)} %copy.13.inc_h, s32[1,4]{1,0:T(1,128)} %req_pages_h.1, s32[1,4]{1,0:T(1,128)} %text_len_h.1, f32[4,1536]{1,0:T(4,128)} %bitcast.5, bf16[512,1536]{1,0:T(8,128)(2,1)} %bitcast.3, bf16[512,1536]{1,0:T(8,128)(2,1)} %bitcast.4, ...), custom_call_target="tpu_custom_call" | custom-call | flops 14000000000 | bytes 10000000 | tf_op jit(solution)/shard_map/pallas_call | solution.py:688
  86.1 0.7 copy.14

commit v6 on v5

--- a/solution.py
+++ b/solution.py
@@ -171,6 +171,8 @@
     def two_first(item, src=None):
         two_go(item, 1, 0, up2, src)
         two_go(item, 4, 0, down2, src)
+
+    def two_near(item, src=None):
         two_go(item, 0, 0, up, src)
         two_go(item, 3, 0, down, src)
 
@@ -342,14 +344,13 @@
         return remote(pick_out.at[kind, cc], pick_in.at[kind, slot], set_send.at[kind, cc], set_recv.at[kind, slot], dev)
 
     def route_send(ring, kind, want):
-        for col in range(0, WIDTH, 512):
-            accs = [jnp.zeros((PAGE, 512), F32)] * 4
-            for zz in range(NZ):
-                page = ring[zz, :, col:col + 512].astype(F32)
-                accs = [jnp.where(want(zz, cc), page, accs[cc]) for cc in range(4)]
-            for cc in range(4):
-                pick_out[kind, cc, :, col:col + 512] = accs[cc].astype(BF16)
         for cc in range(4):
+            wanted = [want(zz, cc) for zz in range(NZ)]
+            for col in range(0, WIDTH, DIM):
+                acc = jnp.zeros((PAGE, DIM), F32)
+                for zz in range(NZ):
+                    acc = jnp.where(wanted[zz], ring[zz, :, col:col + DIM].astype(F32), acc)
+                pick_out[kind, cc, :, col:col + DIM] = acc.astype(BF16)
             dev, here = route_to(kind, cc)
 
             @pl.when(jnp.logical_not(here))
@@ -376,10 +377,11 @@
                 route_copy(kind, cc, c, dev).wait_send()
 
     def want_in(zz, cc):
-        return ints[z * 4 + cc, 0:1, 0:1] == zz * 4 + c
+        return jnp.broadcast_to(ints[z * 4 + cc, 0:1, :], (PAGE, DIM)) == zz * 4 + c
 
     remote(yhi_w(0), yhi_w(0), cross_send.at[NZ], cross_recv.at[NZ], cross).wait_recv()
     z_first(2, yhi_w)
+    two_near(0, lat.at[pl.ds(KEEP, PAGE), :])
     z_step(1, own_w, 1, True)
     y_go(-1)
     y_go(1)
@@ -639,7 +641,9 @@
     back[z, :, WIDTH:] = jnp.full((PAGE, TAG), inc[0, 0], jnp.int32).astype(F32).astype(BF16)
 
     two_first(3)
-    lax.fori_loop(2, 6, step_two, 0)
+    lax.fori_loop(2, 4, step_two, 0)
+    two_near(3)
+    lax.fori_loop(4, 6, step_two, 0)
     two_second(3)
     take_heads(fin, aa_recv)
     gated(home, pl.ds(0, KEEP), p * TOK, [fin[h] for h in range(HEADS)], own_ends, gate)
@@ -647,7 +651,7 @@
     two_last(3)
 
     def want_back(zz, cc):
-        return back[zz, :, WIDTH:WIDTH + 1].astype(F32) == (z * 4 + cc).astype(F32)
+        return back[zz, :, WIDTH:].astype(F32) == (z * 4 + cc).astype(F32)
 
     route_send(back, 1, want_back)
     out[KEEP:TOK, :] = route_take(1)

time: 86.9 us -> 88 us (1.013)
  Pallas kernels: 85.5 us -> 86.5 us
    pallas_call x1, Pallas kernels: 85.5 us -> 86.5 us  [shards(): pl.pallas_call(kernel, out_shape=jax.ShapeDtypeStruct((TOK, WIDTH), BF16)...]
where the time goes in v6:
time: 88 us; the launch traced here: 87.9 us
  Pallas kernels  86.5 us (98%)
    pallas_call x1, Pallas kernels, shards(): pl.pallas_call(kernel, out_shape=jax.ShapeDtypeStruct((TOK, WIDTH), BF16)...  86.5 us

profile of v6, /device:TPU:1, one launch (start us, length us, event | category | flops | bytes accessed | tf_op | source)
XLA Modules:
  0.0 87.9 jit_solution(10665237939138468441)
XLA Ops:
  0.7 86.5 %shard_map.109 = bf16[128,1536]{1,0:T(8,128)(2,1)S(1)} custom-call(bf16[128,1536]{1,0:T(8,128)(2,1)} %lat.1, s32[1,1]{1,0:T(1,128)S(6)} %copy.13.inc_h, s32[1,4]{1,0:T(1,128)} %req_pages_h.1, s32[1,4]{1,0:T(1,128)} %text_len_h.1, f32[4,1536]{1,0:T(4,128)} %bitcast.5, bf16[512,1536]{1,0:T(8,128)(2,1)} %bitcast.3, bf16[512,1536]{1,0:T(8,128)(2,1)} %bitcast.4, ...), custom_call_target="tpu_custom_call" | custom-call | flops 14000000000 | bytes 10000000 | tf_op jit(solution)/shard_map/pallas_call | solution.py:692
  87.2 0.7 copy.14
